TPU v7x, 128 devices: a whole 4x4x4 slice. The times are simulated.
128 devices in a mesh: sec: 4 (over y_lo, core), dom: 32 (over y_hi, z, x).
Axes of the slice: x: 4, y: 4 (y_hi: 2, y_lo: 2; y = y_hi * 2 + y_lo), z: 4, core: 2. Of those that a mesh axis runs over, the one named last changes fastest.
Arguments:
- les_state: float32 [4, 3, 512, 8192], P('sec', None, 'dom'), may hold values from -3 to 3
- les_density: float32 [4, 512, 8192], P('sec', 'dom'), may hold values from 0.5 to 2
- far_state: float32 [4, 3, 512, 8192], P('sec', None, 'dom'), may hold values from -3 to 3
- far_density: float32 [4, 512, 8192], P('sec', 'dom'), may hold values from 0.5 to 2
- face_cell: int32 [1048576], P(('sec', 'dom')), may hold values from 0 to 131071
- face_area: float32 [1048576], P(('sec', 'dom')), may hold values from 0.25 to 4
- face_owner: int32 [1048576], P(('sec', 'dom')), may hold values from 0 to 127, as said below
- face_counts: int32 [128], P(('sec', 'dom')), may hold values from 4096 to 8192, as said below
- face_target: int32 [1048576], P(('sec', 'dom')), may hold values from 0 to 131071
Outputs:
- les_final: float32 [4, 3, 512, 8192], P('sec', None, 'dom')
- far_final: float32 [4, 3, 512, 8192], P('sec', None, 'dom')
Inputs may be any that keep to these rules, and one draw needn't show every extreme that they name: `face_owner`: among one device's 8192 face slots every owner that is named is named by exactly 128 slots, and one owner is named by 128 slots of every device. `face_counts`: some device has all 8192 slots live.
All inputs are finite; a program needn't handle non-finite values.
Results may differ from a plain program's by a relative error of at most 0.0003.
Values sent between devices are 32-bit elements; how exact they have to be, the bound alone decides.
A program may use at most 192 MiB of HBM per device.

v0:
```python
import math

import jax
import jax.numpy as jnp
from jax import lax
from jax.sharding import PartitionSpec as P

SUBSTEPS = 5


TIME_STEP = 0.1
LES_STIFF = 1.0
FAR_STIFF = 1.0
FILTER_WEIGHT = 0.5
MEAN_FLOW = 0.3


def extended(cells, sides, width):
    for axis, dim in sides:
        count = lax.axis_size(axis)
        ends = count - 1
        head = lax.slice_in_dim(cells, 0, width, axis=dim)
        tail = lax.slice_in_dim(cells, cells.shape[dim] - width, cells.shape[dim], axis=dim)
        cells = jnp.concatenate(
            [
                lax.ppermute(tail, axis, [(i, (i + 1) % count) for i in range(ends)]),
                cells,
                lax.ppermute(head, axis, [((i + 1) % count, i) for i in range(ends)]),
            ],
            axis=dim,
        )
    return cells


def along_x(padded):
    return (
        8.0 * (padded[..., 3:-1, :] - padded[..., 1:-3, :])
        - (padded[..., 4:, :] - padded[..., :-4, :])
    ) / 12.0


def along_y(field):
    return (
        8.0 * (jnp.roll(field, -1, -1) - jnp.roll(field, 1, -1))
        - (jnp.roll(field, -2, -1) - jnp.roll(field, 2, -1))
    ) / 12.0


def les_update(padded, inv_density):
    centre = padded[..., 2:-2, :]
    dx_all = along_x(padded)
    dy_all = along_y(centre)
    speed_u = centre[..., 0, :, :]
    speed_v = centre[..., 1, :, :]
    rate_u = (
        speed_u * dx_all[..., 0, :, :]
        + speed_v * dy_all[..., 0, :, :]
        + dx_all[..., 2, :, :] * inv_density
    )
    rate_v = (
        speed_u * dx_all[..., 1, :, :]
        + speed_v * dy_all[..., 1, :, :]
        + dy_all[..., 2, :, :] * inv_density
    )
    rate_p = (
        speed_u * dx_all[..., 2, :, :]
        + speed_v * dy_all[..., 2, :, :]
        + LES_STIFF * (dx_all[..., 0, :, :] + dy_all[..., 1, :, :])
    )
    return centre - TIME_STEP * jnp.stack([rate_u, rate_v, rate_p], axis=-3)


def smooth(padded):
    centre = padded[..., 1:-1, :]
    lateral = padded[..., :-2, :] + padded[..., 2:, :] - 2.0 * centre
    across = jnp.roll(centre, 1, -1) + jnp.roll(centre, -1, -1) - 2.0 * centre
    return centre + FILTER_WEIGHT / 4.0 * (lateral + across)


def far_update(padded, inv_density):
    centre = padded[..., 2:-2, :]
    dx_all = along_x(padded)
    dy_all = along_y(centre)
    rate_u = MEAN_FLOW * dx_all[..., 0, :, :] + dx_all[..., 2, :, :] * inv_density
    rate_v = MEAN_FLOW * dx_all[..., 1, :, :] + dy_all[..., 2, :, :] * inv_density
    rate_p = MEAN_FLOW * dx_all[..., 2, :, :] + FAR_STIFF * (
        dx_all[..., 0, :, :] + dy_all[..., 1, :, :]
    )
    return centre - TIME_STEP * jnp.stack([rate_u, rate_v, rate_p], axis=-3)


def owner_ranks(face_owner, is_live, devices):
    face_total = face_owner.shape[0]
    block = math.gcd(face_total, 128)
    block_count = face_total // block
    hits = ((face_owner[:, None] == jnp.arange(devices)[None, :]) & is_live[:, None]).astype(
        jnp.bfloat16
    )
    blocked = hits.reshape(block_count, block, devices)
    lower_ones = (jnp.arange(block)[:, None] >= jnp.arange(block)[None, :]).astype(jnp.bfloat16)
    within = jnp.einsum("ij,bjd->bid", lower_ones, blocked, preferred_element_type=jnp.float32)
    totals = within[:, -1, :]
    offsets = jnp.cumsum(totals, axis=0) - totals
    counted = within + offsets[:, None, :]
    ranking = jnp.sum((counted - 1.0) * blocked.astype(jnp.float32), axis=2)
    return ranking.reshape(face_total).astype(jnp.int32)


def local(
    les_state,
    les_density,
    far_state,
    far_density,
    face_cell,
    face_area,
    face_owner,
    face_counts,
    face_target,
):
    q_now = les_state[0]
    inv_les = 1.0 / les_density[0]
    rows_les = q_now.shape[1]
    width_cols = q_now.shape[2]
    face_total = face_cell.shape[0]
    field_total = jnp.zeros(q_now.shape, jnp.float32)
    for substep in range(SUBSTEPS):
        padded = extended(q_now, (("dom", 1),), 2)
        advanced = les_update(padded, inv_les)
        q_now = smooth(extended(advanced, (("dom", 1),), 1))
        field_total = field_total + q_now
    summed = jnp.take(field_total.reshape(3, rows_les * width_cols), face_cell, axis=1)
    surface = summed / SUBSTEPS * face_area[None, :]
    devices = lax.axis_size("sec") * lax.axis_size("dom")
    per_owner = 2 * face_total // devices
    slot_total = devices * per_owner
    is_live = jnp.arange(face_total) < face_counts[0]
    ranking = owner_ranks(face_owner, is_live, devices)
    places = jnp.where(is_live, face_owner * per_owner + ranking, slot_total)
    slot_face = (
        jnp.full((slot_total,), face_total, jnp.int32)
        .at[places]
        .set(jnp.arange(face_total, dtype=jnp.int32), mode="drop")
    )
    payload = jnp.concatenate([surface, face_target.astype(jnp.float32)[None, :]], axis=0)
    empty_column = jnp.array([0.0, 0.0, 0.0, -1.0], jnp.float32)[:, None]
    payload = jnp.concatenate([payload, empty_column], axis=1)
    buffer = jnp.take(payload, slot_face, axis=1)
    arrived = lax.all_to_all(buffer, ("sec", "dom"), split_axis=1, concat_axis=1, tiled=True)
    inv_far = 1.0 / far_density[0]
    padded_far = extended(far_state[0], (("dom", 1),), 2)
    stepped = far_update(padded_far, inv_far)
    far_flat = stepped.reshape(3, stepped.shape[1] * stepped.shape[2])
    cell_total = far_flat.shape[1]
    targets = arrived[3].astype(jnp.int32)
    targets = jnp.where(targets >= 0, targets, cell_total)
    far_flat = far_flat.at[:, targets].add(arrived[:3], mode="drop")
    return (q_now[None], far_flat.reshape(stepped.shape)[None])


def solution(mesh):
    placed = (
        P("sec", None, "dom", None),
        P("sec", "dom", None),
        P("sec", None, "dom", None),
        P("sec", "dom", None),
        P(("sec", "dom")),
        P(("sec", "dom")),
        P(("sec", "dom")),
        P(("sec", "dom")),
        P(("sec", "dom")),
    )
    return jax.shard_map(
        local,
        mesh=mesh,
        in_specs=placed,
        out_specs=(P("sec", None, "dom", None), P("sec", None, "dom", None)),
        check_vma=False,
    )
```

profile of v0, /device:TPU:1, one launch (start us, length us, event | category | flops | bytes accessed | tf_op | source)
XLA Modules:
  0.0 840.7 jit_solution(17165052125987141173)
XLA Ops:
  4.3 5.3 collective-permute-start.21
  13.1 4.7 collective-permute-start.1
  22.0 3.9 copy.52
  35.4 9.2 %fusion.9 = f32[64,128,128]{2,1,0:T(8,128)S(1)} fusion(s32[64,128]{1,0:T(8,128)S(1)} %bitcast.86, pred[64,128]{1,0:T(8,128)(4,1)S(1)} %add_compare_fusion), kind=kOutput, calls=%fused_computation.37 | convolution fusion | flops 270548992 | bytes 4235264 | tf_op jit(solution)/shard_map/ij,bjd->bid/dot_general | solution.py:101
  44.6 4.1 multiply_reduce_fusion
  48.7 30.5 %scatter_custom_fusion = s32[16384]{0:T(1024)S(1)} fusion(s32[8192]{0:T(1024)S(1)} %compare_select_fusion.4, s32[8192]{0:T(1024)S(1)} %iota.43, s32[]{:T(128)} %constant.69.clone.1), kind=kCustom, calls=%fused_computation.251 | custom fusion | bytes 65540 | tf_op jit(solution)/shard_map/scatter | solution.py:142
  80.9 3.9 fusion.109
  103.1 6.1 collective-permute-start.5
  114.0 4.9 collective-permute-start.6
  120.5 4.5 collective-permute-done.7
  128.5 5.6 collective-permute-start.9
  138.7 5.9 collective-permute-start.10
  146.2 5.9 collective-permute-done.11
  155.6 6.1 collective-permute-start.13
  166.5 5.9 collective-permute-start.14
  174.0 5.9 collective-permute-done.15
  183.4 6.5 collective-permute-start.17
  194.3 5.9 collective-permute-start.18
  201.8 5.9 collective-permute-done.19
  210.0 30.0 %copy.43 = f32[3,16,8192]{0,2,1:T(8,128)} copy(f32[3,16,8192]{2,1,0:T(8,128)S(1)} %get-tuple-element.14) | data formatting | bytes 3145728 | tf_op jit(solution)/shard_map/add | solution.py:130
  240.0 118.3 %gather_fusion = f32[8192,3]{1,0:T(8,128)} fusion(f32[3,131072]{0,1:T(8,128)} %bitcast.12, s32[8192]{0:T(1024)S(1)} %fusion.143), kind=kCustom, calls=%fused_computation | custom fusion | bytes 229376 | tf_op jit(solution)/shard_map/jit(_take)/gather | solution.py:131
  358.3 9.7 %multiply_bitcast_fusion = f32[3,8192]{0,1:T(8,128)} fusion(f32[8192,3]{1,0:T(8,128)} %gather_fusion, f32[8192]{0:T(1024)S(1)} %broadcast_multiply_fusion, pred[8192]{0:T(1024)(128)(4,1)S(1)} %copy-done.15), kind=kLoop, calls=%fused_computation.7 | loop fusion | flops 49152 | bytes 237568 | tf_op jit(solution)/shard_map/mul | solution.py:132
  370.9 3.0 copy.45
  373.9 56.6 %gather_fusion.1 = f32[16384,4]{1,0:T(8,128)} fusion(f32[4,8193]{0,1:T(8,128)} %copy.45, s32[16384]{0:T(1024)S(1)} %fusion.138), kind=kCustom, calls=%fused_computation.1 | custom fusion | bytes 589824 | tf_op jit(solution)/shard_map/jit(_take)/gather | solution.py:147
  430.5 5.6 copy.46
  436.9 84.0 %all-to-all-start = ((f32[4,128,128]{2,0,1:T(4,128)}), f32[4,128,128]{2,0,1:T(4,128)S(1)}, u32[]{:S(2)}, u32[]{:S(2)}) async-start(f32[4,128,128]{2,0,1:T(4,128)} %broadcast_select_fusion), calls=%async_computation | async-start | bytes 524288 | tf_op jit(solution)/shard_map/all_to_all | solution.py:148
  521.0 4.2 fusion.12
  525.2 30.2 %copy.48 = f32[3,131072]{0,1:T(8,128)} copy(f32[3,131072]{1,0:T(4,128)} %fusion.12) | data formatting | bytes 3145728 | tf_op jit(solution)/shard_map/sub | solution.py:89
  555.6 7.1 sort
  562.8 5.1 copy.49
  567.8 236.7 %scatter_custom_fusion.1 = f32[3,131072]{0,1:T(8,128)} fusion(f32[3,131072]{0,1:T(8,128)} %copy.48, s32[16384]{0:T(1024)S(1)} %get-tuple-element.12, f32[16384,3]{1,0:T(8,128)} %copy.49, s32[16384]{0:T(1024)S(1)} %broadcast_clamp_fusion), kind=kCustom, calls=%fused_computation.5 | custom fusion | flops 49152 | bytes 1572864 | tf_op jit(solution)/shard_map/scatter-add | solution.py:156
  804.5 36.0 %copy.50 = f32[1,3,16,8192]{3,2,1,0:T(8,128)} copy(f32[1,3,16,8192]{1,3,2,0:T(8,128)} %bitcast.21) | data formatting | bytes 3145728
  (159 shorter events, 81.5 us)
Async XLA Ops:
  0.6 20.0 %copy-start = (f32[1,3,16,8192]{3,2,1,0:T(8,128)S(1)}, f32[1,3,16,8192]{3,2,1,0:T(8,128)}, u32[]{:S(2)}) copy-start(f32[1,3,16,8192]{3,2,1,0:T(8,128)} %param.10) | copy-start | bytes 4718596
  3.0 91.3 %collective-permute-start.20 = (f32[3,2,8192]{2,1,0:T(2,128)}, f32[3,2,8192]{2,1,0:T(2,128)S(1)}, u32[]{:S(2)}, u32[]{:S(2)}) collective-permute-start(f32[3,2,8192]{2,1,0:T(2,128)} %get-tuple-element.34), channel_id=1, source_target_pairs={{1,0},{2,1},{3,2},{4,3},{5,4},{6,5},{7,6},{8,7},{9,8},{10,9},{11,1... | collective-permute-start | bytes 589832 | tf_op jit(solution)/shard_map/ppermute | solution.py:28
  4.3 90.0 %collective-permute-start.21 = (f32[3,2,8192]{2,1,0:T(2,128)}, f32[3,2,8192]{2,1,0:T(2,128)}, u32[]{:S(2)}, u32[]{:S(2)}) collective-permute-start(f32[3,2,8192]{2,1,0:T(2,128)} %get-tuple-element.35), channel_id=1, source_target_pairs={{0,1},{1,2},{2,3},{3,4},{4,5},{5,6},{6,7},{7,8},{8,9},{9,10},{10,1... | collective-permute-start | bytes 589832 | tf_op jit(solution)/shard_map/ppermute | solution.py:26
  11.8 75.3 %collective-permute-start = (f32[3,2,8192]{2,1,0:T(2,128)}, f32[3,2,8192]{2,1,0:T(2,128)}, u32[]{:S(2)}, u32[]{:S(2)}) collective-permute-start(f32[3,2,8192]{2,1,0:T(2,128)} %get-tuple-element.114), channel_id=1, source_target_pairs={{1,0},{2,1},{3,2},{4,3},{5,4},{6,5},{7,6},{8,7},{9,8},{10,9},{11,1... | collective-permute-start | bytes 589832 | tf_op jit(solution)/shard_map/ppermute | solution.py:28
  13.1 74.0 %collective-permute-start.1 = (f32[3,2,8192]{2,1,0:T(2,128)}, f32[3,2,8192]{2,1,0:T(2,128)}, u32[]{:S(2)}, u32[]{:S(2)}) collective-permute-start(f32[3,2,8192]{2,1,0:T(2,128)} %get-tuple-element.115), channel_id=1, source_target_pairs={{0,1},{1,2},{2,3},{3,4},{4,5},{5,6},{6,7},{7,8},{8,9},{9,10},{10,1... | collective-permute-start | bytes 589832 | tf_op jit(solution)/shard_map/ppermute | solution.py:26
  44.6 36.2 %copy-start.10 = (s32[8192]{0:T(1024)S(1)}, s32[8192]{0:T(1024)}, u32[]{:S(2)}) copy-start(s32[8192]{0:T(1024)} %param.14) | copy-start | bytes 98308
  80.9 4.7 copy-start.7
  80.9 4.7 copy-start.11
  80.9 4.7 copy-start.12
  80.9 4.7 copy-start.13
  80.9 4.7 copy-start.14
  90.7 8.5 %collective-permute-start.2 = (f32[3,1,8192]{2,1,0:T(1,128)S(1)}, f32[3,1,8192]{2,1,0:T(1,128)S(1)}, u32[]{:S(2)}, u32[]{:S(2)}) collective-permute-start(f32[3,1,8192]{2,1,0:T(1,128)S(1)} %get-tuple-element.112), channel_id=1, source_target_pairs={{0,1},{1,2},{2,3},{3,4},{4,5},{5,6},{6,7},{7,8},{8,9},{9,10},{10,1... | collective-permute-start | bytes 294920 | tf_op jit(solution)/shard_map/ppermute | solution.py:26
  92.7 6.8 collective-permute-start.3
  101.8 8.5 %collective-permute-start.4 = (f32[3,2,8192]{2,1,0:T(2,128)S(1)}, f32[3,2,8192]{2,1,0:T(2,128)S(1)}, u32[]{:S(2)}, u32[]{:S(2)}) collective-permute-start(f32[3,2,8192]{2,1,0:T(2,128)S(1)} %get-tuple-element.98), channel_id=1, source_target_pairs={{1,0},{2,1},{3,2},{4,3},{5,4},{6,5},{7,6},{8,7},{9,8},{10,9},{11,1... | collective-permute-start | bytes 589832 | tf_op jit(solution)/shard_map/ppermute | solution.py:28
  103.1 8.7 %collective-permute-start.5 = (f32[3,2,8192]{2,1,0:T(2,128)S(1)}, f32[3,2,8192]{2,1,0:T(2,128)S(1)}, u32[]{:S(2)}, u32[]{:S(2)}) collective-permute-start(f32[3,2,8192]{2,1,0:T(2,128)S(1)} %get-tuple-element.99), channel_id=1, source_target_pairs={{0,1},{1,2},{2,3},{3,4},{4,5},{5,6},{6,7},{7,8},{8,9},{9,10},{10,1... | collective-permute-start | bytes 589832 | tf_op jit(solution)/shard_map/ppermute | solution.py:26
  114.0 6.5 collective-permute-start.6
  118.9 6.1 collective-permute-start.7
  127.2 7.8 collective-permute-start.8
  128.5 8.0 collective-permute-start.9
  138.7 7.5 collective-permute-start.10
  144.6 7.5 collective-permute-start.11
  154.3 8.5 %collective-permute-start.12 = (f32[3,2,8192]{2,1,0:T(2,128)S(1)}, f32[3,2,8192]{2,1,0:T(2,128)S(1)}, u32[]{:S(2)}, u32[]{:S(2)}) collective-permute-start(f32[3,2,8192]{2,1,0:T(2,128)S(1)} %get-tuple-element.66), channel_id=1, source_target_pairs={{1,0},{2,1},{3,2},{4,3},{5,4},{6,5},{7,6},{8,7},{9,8},{10,9},{11,1... | collective-permute-start | bytes 589832 | tf_op jit(solution)/shard_map/ppermute | solution.py:28
  155.6 8.7 %collective-permute-start.13 = (f32[3,2,8192]{2,1,0:T(2,128)S(1)}, f32[3,2,8192]{2,1,0:T(2,128)S(1)}, u32[]{:S(2)}, u32[]{:S(2)}) collective-permute-start(f32[3,2,8192]{2,1,0:T(2,128)S(1)} %get-tuple-element.67), channel_id=1, source_target_pairs={{0,1},{1,2},{2,3},{3,4},{4,5},{5,6},{6,7},{7,8},{8,9},{9,10},{10,1... | collective-permute-start | bytes 589832 | tf_op jit(solution)/shard_map/ppermute | solution.py:26
  166.5 7.5 collective-permute-start.14
  172.4 7.5 collective-permute-start.15
  182.1 9.6 %collective-permute-start.16 = (f32[3,2,8192]{2,1,0:T(2,128)S(1)}, f32[3,2,8192]{2,1,0:T(2,128)S(1)}, u32[]{:S(2)}, u32[]{:S(2)}) collective-permute-start(f32[3,2,8192]{2,1,0:T(2,128)S(1)} %get-tuple-element.50), channel_id=1, source_target_pairs={{1,0},{2,1},{3,2},{4,3},{5,4},{6,5},{7,6},{8,7},{9,8},{10,9},{11,1... | collective-permute-start | bytes 589832 | tf_op jit(solution)/shard_map/ppermute | solution.py:28
  183.4 8.7 %collective-permute-start.17 = (f32[3,2,8192]{2,1,0:T(2,128)S(1)}, f32[3,2,8192]{2,1,0:T(2,128)S(1)}, u32[]{:S(2)}, u32[]{:S(2)}) collective-permute-start(f32[3,2,8192]{2,1,0:T(2,128)S(1)} %get-tuple-element.51), channel_id=1, source_target_pairs={{0,1},{1,2},{2,3},{3,4},{4,5},{5,6},{6,7},{7,8},{8,9},{9,10},{10,1... | collective-permute-start | bytes 589832 | tf_op jit(solution)/shard_map/ppermute | solution.py:26
  194.3 7.5 collective-permute-start.18
  200.2 7.5 collective-permute-start.19
  210.0 148.3 %copy-start.15 = (pred[8192]{0:T(1024)(128)(4,1)S(1)}, pred[8192]{0:T(1024)(128)(4,1)}, u32[]{:S(2)}) copy-start(pred[8192]{0:T(1024)(128)(4,1)} %compare_and_fusion) | copy-start | bytes 24580
  430.5 90.5 %copy-start.3 = (f32[1,3,16,8192]{3,1,2,0:T(4,128)S(1)}, f32[1,3,16,8192]{3,1,2,0:T(4,128)}, u32[]{:S(2)}) copy-start(f32[1,3,16,8192]{3,1,2,0:T(4,128)} %copy.52) | copy-start | bytes 4718596
  436.9 118.4 %all-to-all-start = ((f32[4,128,128]{2,0,1:T(4,128)}), f32[4,128,128]{2,0,1:T(4,128)S(1)}, u32[]{:S(2)}, u32[]{:S(2)}) async-start(f32[4,128,128]{2,0,1:T(4,128)} %broadcast_select_fusion), calls=%async_computation | async-start | bytes 524288 | tf_op jit(solution)/shard_map/all_to_all | solution.py:148
  (8 other events, 27.8 us)
where the time goes:
time: 856 us; the launch traced here: 841 us
  local copies, waits for them, and re-layouts  352 us (41%)
  other arithmetic  290 us (34%)
  starting transfers between devices  157 us (18%)
  waiting for transfers between devices  29.5 us (3%)
  matrix products  9.15 us (1%)
    scatter-add x3, other arithmetic, local(): far_flat = far_flat.at[:, targets].add(arrived[:3], mode='drop')  244 us
    gather x1, local copies, waits for them, and re-layouts, local(): jnp.take(field_total.reshape(3, rows_les * width_cols), face_cell, axis=1)  118 us
    all_to_all x1, starting transfers between devices, local(): lax.all_to_all(buffer, ('sec', 'dom'), split_axis=1, concat_axis=1, tiled...  84 us
    gather x2, local copies, waits for them, and re-layouts, local(): buffer = jnp.take(payload, slot_face, axis=1)  62.2 us
    ppermute x11, starting transfers between devices, extended(): lax.ppermute(tail, axis, [(i, (i + 1) % count) for i in range(ends)])  58.9 us
    unnamed x39, local copies, waits for them, and re-layouts  43.1 us
    scatter x1, local copies, waits for them, and re-layouts, local(): slot_face = jnp.full((slot_total,), face_total, jnp.int32).at[places].set...  30.5 us
    sub x1, local copies, waits for them, and re-layouts, far_update(): return centre - TIME_STEP * jnp.stack([rate_u, rate_v, rate_p], axis=-3)  30.2 us
  transfers between devices with their start and end apart: 23, of which 16 were waited for; matrix products, arithmetic and copies ran while one was open for 14% of the time, Pallas kernels for 0%

commit v1 on v0

v1 whole, which is shorter than its diff:
```python
import jax
import jax.numpy as jnp
from jax import lax
from jax.experimental import pallas as pl
from jax.experimental.pallas import tpu as pltpu
from jax.sharding import PartitionSpec as P

SUBSTEPS = 5
TIME_STEP = 0.1
LES_STIFF = 1.0
FAR_STIFF = 1.0
FILTER_WEIGHT = 0.5
MEAN_FLOW = 0.3

LANES = 128
TILE = 8
ROWS = 16
COLS = 8192
TILES = COLS // LANES
REGS = TILES // TILE
FACES = 8192
FACE_ROWS = FACES // LANES
DEVICES = 128
RANKS = 128
CELL_ROWS = ROWS * COLS // LANES

MESH = pl.DeviceIdType.MESH
VMEM = pl.BlockSpec(memory_space=pltpu.VMEM)
SMEM = pl.BlockSpec(memory_space=pltpu.SMEM)
F32 = jnp.float32
BF16 = jnp.bfloat16
I32 = jnp.int32


def params(**more):
    return pltpu.CompilerParams(vmem_limit_bytes=56 * 1024 * 1024, **more)


def rows_from_tiles(load, flat, store, rows8):
    for block in range(TILES):
        flat[block * TILE : (block + 1) * TILE, :] = load(block)
    for row in range(TILE):
        for reg in range(REGS):
            store(rows8 * TILE + row, reg, flat[pl.ds(TILE * reg + row, TILE, stride=TILES), :])


def tiles_from_rows(load, flat, store, rows8):
    for row in range(TILE):
        for reg in range(REGS):
            flat[pl.ds(TILE * reg + row, TILE, stride=TILES), :] = load(rows8 * TILE + row, reg)
    for block in range(TILES):
        store(block, flat[block * TILE : (block + 1) * TILE, :])


def shifted(row, by, lane):
    if by > 0:
        turned = pltpu.roll(row, LANES - by, 1)
        crossed = jnp.concatenate([turned[TILE:], pltpu.roll(turned[:TILE], TILE - 1, 0)], axis=0)
        return jnp.where(lane >= LANES - by, crossed, turned)
    turned = pltpu.roll(row, -by, 1)
    crossed = jnp.concatenate(
        [pltpu.roll(turned[TILES - TILE :], 1, 0), turned[: TILES - TILE]], axis=0
    )
    return jnp.where(lane < -by, crossed, turned)


def difference(far_left, left, right, far_right):
    return 8.0 * (right - left) - (far_right - far_left)


def across(row, lane):
    return difference(
        shifted(row, -2, lane), shifted(row, -1, lane), shifted(row, 1, lane), shifted(row, 2, lane)
    )


def fields_kernel(
    les_ref,
    les_density_ref,
    far_ref,
    far_density_ref,
    les_out,
    total_out,
    stepped_out,
    state,
    advanced,
    inverse,
    far,
    far_inverse,
    flat,
    send_sem,
    recv_sem,
    inverse_send,
    inverse_recv,
    far_send,
    far_recv,
):
    dom = lax.axis_index("dom")
    doms = lax.axis_size("dom")
    has_up = dom > 0
    has_down = dom < doms - 1
    up = lax.rem(dom + doms - 1, doms)
    down = lax.rem(dom + 1, doms)
    lane = lax.broadcasted_iota(I32, (TILES, LANES), 1)
    step = TIME_STEP / 12.0

    barrier = pltpu.get_barrier_semaphore()

    @pl.when(has_up)
    def _():
        pl.semaphore_signal(barrier, inc=1, device_id={"dom": up}, device_id_type=MESH)

    @pl.when(has_down)
    def _():
        pl.semaphore_signal(barrier, inc=1, device_id={"dom": down}, device_id_type=MESH)

    def remote(ref, first, count, landing, sems, where):
        return pltpu.make_async_remote_copy(
            src_ref=ref.at[pl.ds(first, count)],
            dst_ref=ref.at[pl.ds(landing, count)],
            send_sem=sems[0],
            recv_sem=sems[1],
            device_id={"dom": where},
            device_id_type=MESH,
        )

    def up_copy(sub):
        sems = (send_sem.at[sub, 0], recv_sem.at[sub, 0])
        return remote(state.at[sub], 3, 3, ROWS + 3, sems, up)

    def down_copy(sub):
        sems = (send_sem.at[sub, 1], recv_sem.at[sub, 1])
        return remote(state.at[sub], ROWS, 3, 0, sems, down)

    def inverse_up():
        return remote(inverse, 1, 1, ROWS + 1, (inverse_send.at[0], inverse_recv.at[0]), up)

    def inverse_down():
        return remote(inverse, ROWS, 1, 0, (inverse_send.at[1], inverse_recv.at[1]), down)

    def far_up():
        return remote(far, 2, 2, ROWS + 2, (far_send.at[0], far_recv.at[0]), up)

    def far_down():
        return remote(far, ROWS, 2, 0, (far_send.at[1], far_recv.at[1]), down)

    @pl.when(jnp.logical_not(has_up))
    def _():
        for sub in range(SUBSTEPS):
            state[sub, 0:3] = jnp.zeros((3, 3, TILES, LANES), F32)
        inverse[0] = jnp.zeros((TILES, LANES), F32)
        far[0:2] = jnp.zeros((2, 3, TILES, LANES), F32)

    @pl.when(jnp.logical_not(has_down))
    def _():
        for sub in range(SUBSTEPS):
            state[sub, ROWS + 3 :] = jnp.zeros((3, 3, TILES, LANES), F32)
        inverse[ROWS + 1] = jnp.zeros((TILES, LANES), F32)
        far[ROWS + 2 : ROWS + 4] = jnp.zeros((2, 3, TILES, LANES), F32)

    def convert_state(source, target, offset):
        @pl.loop(0, 6)
        def _(index):
            part, rows8 = index // 2, index % 2

            def load(block):
                return source[part, pl.ds(rows8 * TILE, TILE), block * LANES : (block + 1) * LANES]

            def store(row, reg, value):
                target[offset + row, part, reg * TILE : (reg + 1) * TILE, :] = value

            rows_from_tiles(load, flat, store, rows8)

    def convert_density(source, target, offset):
        @pl.loop(0, 2)
        def _(rows8):
            def load(block):
                return 1.0 / source[pl.ds(rows8 * TILE, TILE), block * LANES : (block + 1) * LANES]

            def store(row, reg, value):
                target[offset + row, reg * TILE : (reg + 1) * TILE, :] = value

            rows_from_tiles(load, flat, store, rows8)

    def advance(sub, row):
        base = row + 3
        u, v, p = (state[sub, base, part] for part in range(3))
        dx = [
            difference(*(state[sub, base + by, part] for by in (-2, -1, 1, 2)))
            for part in range(3)
        ]
        dy = [across(field, lane) for field in (u, v, p)]
        inv = inverse[row + 1]
        rate_u = u * dx[0] + v * dy[0] + inv * dx[2]
        rate_v = u * dx[1] + v * dy[1] + inv * dy[2]
        rate_p = u * dx[2] + v * dy[2] + LES_STIFF * (dx[0] + dy[1])
        return u - step * rate_u, v - step * rate_v, p - step * rate_p

    def put_advanced(row, fields):
        for part in range(3):
            advanced[row + 1, part] = fields[part]

    def smooth(sub, row):
        for part in range(3):
            centre = advanced[row + 1, part]
            lateral = advanced[row, part] + advanced[row + 2, part]
            sides = shifted(centre, 1, lane) + shifted(centre, -1, lane)
            value = (1.0 - FILTER_WEIGHT) * centre + FILTER_WEIGHT / 4.0 * (lateral + sides)
            state[sub + 1, row + 3, part] = value
            if sub == 0:
                total_out[part, row] = value
            else:
                total_out[part, row] += value

    def far_row(row):
        base = row + 2
        u, v, p = (far[base, part] for part in range(3))
        dx = [
            difference(*(far[base + by, part] for by in (-2, -1, 1, 2))) for part in range(3)
        ]
        inv = far_inverse[row]
        dy_v, dy_p = across(v, lane), across(p, lane)
        far[base + ROWS + 4, 0] = u - step * (MEAN_FLOW * dx[0] + inv * dx[2])
        far[base + ROWS + 4, 1] = v - step * (MEAN_FLOW * dx[1] + inv * dy_p)
        far[base + ROWS + 4, 2] = p - step * (MEAN_FLOW * dx[2] + FAR_STIFF * (dx[0] + dy_v))

    def loop(low, high, body):
        @pl.loop(low, high)
        def _(row):
            body(row)

    def write_tiles(source, target):
        @pl.loop(0, 6)
        def _(index):
            part, rows8 = index // 2, index % 2

            def load(row, reg):
                return source(row, part, reg)

            def store(block, value):
                target[part, pl.ds(rows8 * TILE, TILE), block * LANES : (block + 1) * LANES] = value

            tiles_from_rows(load, flat, store, rows8)

    convert_state(les_ref, state.at[0], 3)
    convert_density(les_density_ref, inverse, 1)

    pl.semaphore_wait(barrier, jnp.where(has_up, 1, 0) + jnp.where(has_down, 1, 0))

    @pl.when(has_up)
    def _():
        up_copy(0).start()
        inverse_up().start()

    @pl.when(has_down)
    def _():
        down_copy(0).start()
        inverse_down().start()

    for sub in range(SUBSTEPS):
        loop(2, ROWS - 2, lambda row: put_advanced(row, advance(sub, row)))
        loop(3, ROWS - 3, lambda row: smooth(sub, row))
        if sub == 0:
            convert_state(far_ref, far, 2)
            convert_density(far_density_ref, far_inverse, 0)
        if sub == 1:
            loop(2, ROWS - 2, far_row)

        @pl.when(has_up)
        def _():
            down_copy(sub).wait_recv()
            if sub == 0:
                inverse_down().wait_recv()

        loop(0, 2, lambda row: put_advanced(row, advance(sub, row)))
        put_advanced(-1, [jnp.where(has_up, field, 0.0) for field in advance(sub, -1)])
        loop(0, 3, lambda row: smooth(sub, row))

        if sub < SUBSTEPS - 1:

            @pl.when(has_up)
            def _():
                up_copy(sub + 1).start()

        @pl.when(has_down)
        def _():
            up_copy(sub).wait_recv()
            if sub == 0:
                inverse_up().wait_recv()

        loop(ROWS - 2, ROWS, lambda row: put_advanced(row, advance(sub, row)))
        put_advanced(ROWS, [jnp.where(has_down, field, 0.0) for field in advance(sub, ROWS)])
        loop(ROWS - 3, ROWS, lambda row: smooth(sub, row))

        if sub < SUBSTEPS - 1:

            @pl.when(has_down)
            def _():
                down_copy(sub + 1).start()

        if sub == SUBSTEPS - 2:

            @pl.when(has_up)
            def _():
                far_up().start()

            @pl.when(has_down)
            def _():
                far_down().start()

    write_tiles(
        lambda row, part, reg: state[SUBSTEPS, row + 3, part, reg * TILE : (reg + 1) * TILE, :],
        les_out,
    )

    @pl.when(has_up)
    def _():
        far_down().wait_recv()

    @pl.when(has_down)
    def _():
        far_up().wait_recv()

    loop(0, 2, far_row)
    loop(ROWS - 2, ROWS, far_row)
    write_tiles(
        lambda row, part, reg: far[row + ROWS + 6, part, reg * TILE : (reg + 1) * TILE, :],
        stepped_out,
    )

    @pl.when(has_up)
    def _():
        for sub in range(SUBSTEPS):
            up_copy(sub).wait_send()
        inverse_up().wait_send()
        far_up().wait_send()

    @pl.when(has_down)
    def _():
        for sub in range(SUBSTEPS):
            down_copy(sub).wait_send()
        inverse_down().wait_send()
        far_down().wait_send()


def fields(les_state, les_density, far_state, far_density):
    block = jax.ShapeDtypeStruct((3, ROWS, COLS), F32)
    return pl.pallas_call(
        fields_kernel,
        out_shape=(block, jax.ShapeDtypeStruct((3, ROWS, TILES, LANES), F32), block),
        in_specs=[VMEM] * 4,
        out_specs=(VMEM,) * 3,
        scratch_shapes=[
            pltpu.VMEM((SUBSTEPS + 1, ROWS + 6, 3, TILES, LANES), F32),
            pltpu.VMEM((ROWS + 2, 3, TILES, LANES), F32),
            pltpu.VMEM((ROWS + 2, TILES, LANES), F32),
            pltpu.VMEM((2 * ROWS + 6, 3, TILES, LANES), F32),
            pltpu.VMEM((ROWS, TILES, LANES), F32),
            pltpu.VMEM((TILES * TILE, LANES), F32),
            pltpu.SemaphoreType.DMA((SUBSTEPS, 2)),
            pltpu.SemaphoreType.DMA((SUBSTEPS, 2)),
            pltpu.SemaphoreType.DMA((2,)),
            pltpu.SemaphoreType.DMA((2,)),
            pltpu.SemaphoreType.DMA((2,)),
            pltpu.SemaphoreType.DMA((2,)),
        ],
        compiler_params=params(collective_id=0, has_side_effects=True),
        name="fields",
    )(les_state, les_density, far_state, far_density)


RANK_BLOCK = 256


def rank_kernel(count_ref, owner_ref, rank_out):
    live = count_ref[0]
    owners = lax.broadcasted_iota(I32, (DEVICES, RANK_BLOCK), 0)
    before = lax.broadcasted_iota(I32, (RANK_BLOCK, RANK_BLOCK), 0)
    after = lax.broadcasted_iota(I32, (RANK_BLOCK, RANK_BLOCK), 1)
    weights = jnp.concatenate(
        [
            jnp.where(before < after, 1.0, 0.0).astype(BF16),
            jnp.ones((RANK_BLOCK, RANK_BLOCK), BF16),
        ],
        axis=1,
    )
    place = lax.broadcasted_iota(I32, (1, RANK_BLOCK), 1)
    base = jnp.zeros((DEVICES, RANK_BLOCK), F32)
    wide = RANK_BLOCK // LANES
    for block in range(FACES // RANK_BLOCK):
        rows = [owner_ref[block * wide + i : block * wide + i + 1, :] for i in range(wide)]
        named = jnp.concatenate(rows, axis=1)
        is_live = place + block * RANK_BLOCK < live
        named = jnp.where(is_live, named, -1)
        hits = jnp.where(owners == named, 1.0, 0.0)
        counted = jnp.dot(hits.astype(BF16), weights, preferred_element_type=F32)
        rank = jnp.sum(hits * (counted[:, :RANK_BLOCK] + base), axis=0, keepdims=True)
        base = base + counted[:, RANK_BLOCK:]
        rank = jnp.where(is_live, rank.astype(I32), -1)
        for i in range(wide):
            rank_out[block * wide + i : block * wide + i + 1, :] = rank[
                :, i * LANES : (i + 1) * LANES
            ]


def ranks(counts, owner):
    return pl.pallas_call(
        rank_kernel,
        out_shape=jax.ShapeDtypeStruct((FACE_ROWS, LANES), I32),
        in_specs=[SMEM, VMEM],
        out_specs=VMEM,
        compiler_params=params(),
        name="ranks",
    )(counts, owner)


def halves(values):
    high = values.astype(BF16).astype(F32)
    return high, values - high


PICK = 512


def pick_kernel(total_ref, cell_ref, area_ref, owner_ref, target_ref, rank_ref, out, turned, slots):
    for part in range(3):
        for block in range(CELL_ROWS // LANES):
            columns = slice(block * LANES, (block + 1) * LANES)
            high, low = halves(total_ref[part, columns, :].T)
            turned[2 * part * LANES : (2 * part + 1) * LANES, columns] = high.astype(BF16)
            turned[(2 * part + 1) * LANES : (2 * part + 2) * LANES, columns] = low.astype(BF16)
    slots[...] = jnp.zeros_like(slots)
    wide = PICK // LANES
    cell_rows = lax.broadcasted_iota(I32, (CELL_ROWS, PICK), 0)
    index = lax.broadcasted_iota(I32, (LANES, PICK), 0)

    @pl.loop(0, FACES // PICK)
    def _(block):
        def line(ref):
            return jnp.concatenate([ref[pl.ds(block * wide + i, 1), :] for i in range(wide)], axis=1)

        cell, area, owner, target, rank = (
            line(ref) for ref in (cell_ref, area_ref, owner_ref, target_ref, rank_ref)
        )
        row, column = cell >> 13, cell & (COLS - 1)
        cell_row = row * TILES + ((column >> 7) & 7) * TILE + (column >> 10)
        picked = jnp.where(cell_rows == cell_row, 1.0, 0.0).astype(BF16)
        found = jnp.dot(turned[...], picked, preferred_element_type=F32)
        is_lane = index == (column & (LANES - 1))
        is_rank = index == rank
        parts = []
        for part in range(3):
            both = (
                found[2 * part * LANES : (2 * part + 1) * LANES]
                + found[(2 * part + 1) * LANES : (2 * part + 2) * LANES]
            )
            value = jnp.sum(jnp.where(is_lane, both, 0.0), axis=0, keepdims=True)
            parts.extend(halves(value * (area * (1.0 / SUBSTEPS))))
        for shift in (0, 7, 14):
            parts.append(((target >> shift) & (LANES - 1)).astype(F32))
        spread = jnp.concatenate(
            [jnp.where(is_rank, part, 0.0).astype(BF16) for part in parts], axis=0
        )
        named = jnp.where(index == owner, 1.0, 0.0).astype(BF16)
        slots[...] += lax.dot_general(
            named, spread, (((1,), (1,)), ((), ())), preferred_element_type=F32
        )

    pieces = [slots[:, i * LANES : (i + 1) * LANES] for i in range(9)]
    for part in range(3):
        out[pl.ds(part, DEVICES, stride=4), :] = pieces[2 * part] + pieces[2 * part + 1]
    out[pl.ds(3, DEVICES, stride=4), :] = (
        pieces[6] + pieces[7] * float(LANES) + pieces[8] * float(LANES * LANES)
    )


def pick(total, cell, area, owner, target, rank):
    return pl.pallas_call(
        pick_kernel,
        out_shape=jax.ShapeDtypeStruct((4 * DEVICES, LANES), F32),
        in_specs=[VMEM] * 6,
        out_specs=VMEM,
        scratch_shapes=[
            pltpu.VMEM((6 * LANES, CELL_ROWS), BF16),
            pltpu.VMEM((DEVICES, 9 * LANES), F32),
        ],
        compiler_params=params(),
        name="pick",
    )(total, cell, area, owner, target, rank)


def exchange_kernel(ready, arrived, local_sem, send_sem, recv_sem):
    secs, doms = lax.axis_size("sec"), lax.axis_size("dom")
    devices = secs * doms
    me = lax.axis_index("sec") * doms + lax.axis_index("dom")
    barrier = pltpu.get_barrier_semaphore()

    def place(offset):
        other = lax.rem(me + offset, devices)
        return other, {"sec": other // doms, "dom": lax.rem(other, doms)}

    @pl.loop(1, devices)
    def _(offset):
        pl.semaphore_signal(barrier, inc=1, device_id=place(offset)[1], device_id_type=MESH)

    own = pltpu.make_async_copy(ready.at[me], arrived.at[me], local_sem)
    own.start()
    pl.semaphore_wait(barrier, devices - 1)

    @pl.loop(1, devices)
    def _(offset):
        other, where = place(offset)
        pltpu.make_async_remote_copy(
            src_ref=ready.at[other],
            dst_ref=arrived.at[me],
            send_sem=send_sem,
            recv_sem=recv_sem,
            device_id=where,
            device_id_type=MESH,
        ).start()

    own.wait()
    all_but_one = pl.ds(0, devices - 1)
    pltpu.make_async_copy(arrived.at[all_but_one], arrived.at[all_but_one], recv_sem).wait()
    pltpu.make_async_copy(ready.at[all_but_one], ready.at[all_but_one], send_sem).wait()


def exchange(ready):
    return pl.pallas_call(
        exchange_kernel,
        out_shape=jax.ShapeDtypeStruct(ready.shape, F32),
        in_specs=[VMEM],
        out_specs=VMEM,
        scratch_shapes=[pltpu.SemaphoreType.DMA] * 3,
        compiler_params=params(collective_id=1, has_side_effects=True),
        name="exchange",
    )(ready)


ADD = 512


def add_kernel(arrived_ref, stepped_ref, out, held, sums):
    for part in range(4):
        held[part] = arrived_ref[pl.ds(part, DEVICES, stride=4), :]
    sums[...] = jnp.zeros_like(sums)
    wide = ADD // LANES
    cell_rows = lax.broadcasted_iota(I32, (CELL_ROWS, ADD), 0)
    index = lax.broadcasted_iota(I32, (LANES, ADD), 0)

    @pl.loop(0, DEVICES * RANKS // ADD)
    def _(block):
        def line(part):
            return jnp.concatenate(
                [held[part, pl.ds(block * wide + i, 1), :] for i in range(wide)], axis=1
            )

        target = line(3).astype(I32)
        row, column = target >> 13, target & (COLS - 1)
        cell_row = ((row >> 3) * TILES + (column >> 7)) * TILE + (row & 7)
        hits = jnp.where(cell_rows == cell_row, 1.0, 0.0).astype(BF16)
        is_lane = index == (column & (LANES - 1))
        parts = [half for part in range(3) for half in halves(line(part))]
        spread = jnp.concatenate(
            [jnp.where(is_lane, part, 0.0).astype(BF16) for part in parts], axis=0
        )
        sums[...] += lax.dot_general(
            hits, spread, (((1,), (1,)), ((), ())), preferred_element_type=F32
        )

    for part in range(3):
        high = slice(2 * part * LANES, (2 * part + 1) * LANES)
        low = slice((2 * part + 1) * LANES, (2 * part + 2) * LANES)
        for band in range(ROWS // TILE):
            rows = slice(band * TILE, (band + 1) * TILE)
            for block in range(TILES):
                first = (band * TILES + block) * TILE
                columns = slice(block * LANES, (block + 1) * LANES)
                out[part, rows, columns] = stepped_ref[part, rows, columns] + (
                    sums[first : first + TILE, high] + sums[first : first + TILE, low]
                )


def add(arrived, stepped):
    return pl.pallas_call(
        add_kernel,
        out_shape=jax.ShapeDtypeStruct((3, ROWS, COLS), F32),
        in_specs=[VMEM] * 2,
        out_specs=VMEM,
        scratch_shapes=[
            pltpu.VMEM((4, DEVICES, RANKS), F32),
            pltpu.VMEM((CELL_ROWS, 6 * LANES), F32),
        ],
        compiler_params=params(),
        name="add",
    )(arrived, stepped)


def local(
    les_state,
    les_density,
    far_state,
    far_density,
    face_cell,
    face_area,
    face_owner,
    face_counts,
    face_target,
):
    cell, area, owner, target = (
        array.reshape(FACE_ROWS, LANES) for array in (face_cell, face_area, face_owner, face_target)
    )
    rank = ranks(face_counts, owner)
    les_final, total, stepped = fields(les_state[0], les_density[0], far_state[0], far_density[0])
    ready = pick(total.reshape(3, CELL_ROWS, LANES), cell, area, owner, target, rank)
    arrived = exchange(ready.reshape(DEVICES, 4, LANES))
    far_final = add(arrived.reshape(4 * DEVICES, LANES), stepped)
    return les_final[None], far_final[None]


def solution(mesh):
    field = P("sec", None, "dom", None)
    density = P("sec", "dom", None)
    faces = P(("sec", "dom"))
    return jax.shard_map(
        local,
        mesh=mesh,
        in_specs=(field, density, field, density) + (faces,) * 5,
        out_specs=(field, field),
        check_vma=False,
    )
```

time: 856 us -> 153 us (0.18); the launches traced: 841 us -> 153 us
  local copies, waits for them, and re-layouts: 352 us -> 1.15 us
  other arithmetic: 290 us -> 0 us
  starting transfers between devices: 157 us -> 0 us
  Pallas kernels: 0 us -> 151 us
  waiting for transfers between devices: 29.5 us -> 0 us
  matrix products: 9.15 us -> 0 us
    scatter-add x3 -> x0, other arithmetic: 244 us -> none  [local(): far_flat = far_flat.at[:, targets].add(arrived[:3], mode='drop')]
    gather x3 -> x0, local copies, waits for them, and re-layouts: 181 us -> none  [the longest x1 118 us: local(): jnp.take(field_total.reshape(3, rows_les * width_cols), face_cell, axis=1)]
    pallas_call x0 -> x5, Pallas kernels: none -> 151 us  [the longest x1 48.2 us: fields(): pl.pallas_call(fields_kernel, out_shape=(block, jax.ShapeDtypeStruct((3,...]
    all_to_all x1 -> x0, starting transfers between devices: 84 us -> none  [local(): lax.all_to_all(buffer, ('sec', 'dom'), split_axis=1, concat_axis=1, tiled...]
    ppermute x22 -> x0, starting transfers between devices: 73.4 us -> none  [the longest x11 58.9 us: extended(): lax.ppermute(tail, axis, [(i, (i + 1) % count) for i in range(ends)])]
    unnamed x39 -> x3, local copies, waits for them, and re-layouts: 43.1 us -> 1.15 us
    slice x48 -> x0, local copies, waits for them, and re-layouts: 31.7 us -> none  [the longest x12 8.86 us: along_y(): jnp.roll(field, 2, -1)]
    scatter x1 -> x0, local copies, waits for them, and re-layouts: 30.5 us -> none  [local(): slot_face = jnp.full((slot_total,), face_total, jnp.int32).at[places].set...]
  transfers between devices with their start and end apart: 23 -> 0, of which waited for: 16 -> 0; matrix products, arithmetic and copies ran while one was open for 14% -> 0% of each run, Pallas kernels for 0% -> 0%
where the time goes in v1:
time: 153 us
  Pallas kernels  151 us (99%)
    pallas_call x1, Pallas kernels, fields(): pl.pallas_call(fields_kernel, out_shape=(block, jax.ShapeDtypeStruct((3,...  48.2 us
    pallas_call x1, Pallas kernels, exchange(): pl.pallas_call(exchange_kernel, out_shape=jax.ShapeDtypeStruct(ready.shap...  37.2 us
    pallas_call x1, Pallas kernels, add(): pl.pallas_call(add_kernel, out_shape=jax.ShapeDtypeStruct((3, ROWS, COLS)...  36.3 us
    pallas_call x1, Pallas kernels, pick(): pl.pallas_call(pick_kernel, out_shape=jax.ShapeDtypeStruct((4 * DEVICES,...  25.8 us

profile of v1, /device:TPU:1, one launch (start us, length us, event | category | flops | bytes accessed | tf_op | source)
XLA Modules:
  0.0 153.0 jit_solution(15816977713084619795)
XLA Ops:
  0.6 48.2 %fields.1 = (f32[3,16,8192]{2,1,0:T(8,128)}, f32[3,16,64,128]{3,2,1,0:T(8,128)}, f32[3,16,8192]{2,1,0:T(8,128)}) custom-call(f32[3,16,8192]{2,1,0:T(8,128)} %bitcast.15, f32[16,8192]{1,0:T(8,128)} %bitcast.20, f32[3,16,8192]{2,1,0:T(8,128)} %bitcast.16, f32[16,8192]{1,0:T(8,128)} %bitcast.21), custom_call_target="tpu_custom_call" | custom-call | tf_op jit(solution)/shard_map/fields/pallas_call | solution.py:348
  49.5 3.0 %ranks.1.rank_ref = s32[64,128]{1,0:T(8,128)} custom-call(s32[1]{0:T(128)S(6)} %copy.12.count_ref, s32[64,128]{1,0:T(8,128)} %bitcast.22), custom_call_target="tpu_custom_call" | custom-call | tf_op jit(solution)/shard_map/ranks/pallas_call | solution.py:407
  52.5 25.8 %pick.1 = f32[512,128]{1,0:T(8,128)} custom-call(f32[3,1024,128]{2,1,0:T(8,128)} %bitcast.14, s32[64,128]{1,0:T(8,128)} %bitcast.24, f32[64,128]{1,0:T(8,128)} %bitcast.25, s32[64,128]{1,0:T(8,128)} %bitcast.23, s32[64,128]{1,0:T(8,128)} %bitcast.26, s32[64,128]{1,0:T(8,128)} %ranks.1.rank_ref), custom_call_target="tpu_custom_call" | custom-call | tf_op jit(solution)/shard_map/pick/pallas_call | solution.py:478
  78.3 37.2 %exchange.1 = f32[128,4,128]{2,1,0:T(4,128)} custom-call(f32[128,4,128]{2,1,0:T(4,128)} %bitcast.18), custom_call_target="tpu_custom_call" | custom-call | tf_op jit(solution)/shard_map/exchange/pallas_call | solution.py:529
  115.5 0.0 copy-start
  115.5 36.3 %add.1 = f32[3,16,8192]{2,1,0:T(8,128)} custom-call(f32[512,128]{1,0:T(8,128)} %bitcast.19, f32[3,16,8192]{2,1,0:T(8,128)} %get-tuple-element.7.stepped_ref), custom_call_target="tpu_custom_call" | custom-call | tf_op jit(solution)/shard_map/add/pallas_call | solution.py:585
  151.9 0.0 copy-done
  151.9 1.1 copy.13
Async XLA Ops:
  115.5 36.3 %copy-start = (f32[3,16,8192]{2,1,0:T(8,128)S(1)}, f32[3,16,8192]{2,1,0:T(8,128)}, u32[]{:S(2)}) copy-start(f32[3,16,8192]{2,1,0:T(8,128)} %get-tuple-element.5) | copy-start | bytes 4718596

commit v2 on v1

--- a/solution.py
+++ b/solution.py
@@ -6,6 +6,7 @@
 from jax.sharding import PartitionSpec as P
 
 SUBSTEPS = 5
+UNROLL = {12: 4, 10: 5}
 TIME_STEP = 0.1
 LES_STIFF = 1.0
 FAR_STIFF = 1.0
@@ -225,7 +226,7 @@
         far[base + ROWS + 4, 2] = p - step * (MEAN_FLOW * dx[2] + FAR_STIFF * (dx[0] + dy_v))
 
     def loop(low, high, body):
-        @pl.loop(low, high)
+        @pl.loop(low, high, unroll=UNROLL.get(high - low, high - low))
         def _(row):
             body(row)
 
@@ -370,9 +371,74 @@
 
 
 RANK_BLOCK = 256
-
-
-def rank_kernel(count_ref, owner_ref, rank_out):
+BUCKETS = 4
+BUCKET = CELL_ROWS // BUCKETS
+BLOCK = 256
+LINE = 512
+TOGETHER = 4
+PLANNED = 48
+SORTED = 80
+
+
+def halves(values):
+    high = values.astype(BF16).astype(F32)
+    return high, values - high
+
+
+def indices(rows, columns):
+    return lax.broadcasted_iota(I32, (rows, columns), 0).astype(F32).astype(BF16)
+
+
+def one_hot(index, line):
+    return jnp.where(index == line.astype(BF16), jnp.ones((), BF16), jnp.zeros((), BF16))
+
+
+def spread(index, line, parts):
+    here = index == line.astype(BF16)
+    return jnp.concatenate(
+        [jnp.where(here, part.astype(BF16), jnp.zeros((), BF16)) for part in parts], axis=0
+    )
+
+
+def product(left, right):
+    return lax.dot_general(left, right, (((1,), (1,)), ((), ())), preferred_element_type=F32)
+
+
+def lines(ref, first, count):
+    return jnp.concatenate([ref[pl.ds(first + i, 1), :] for i in range(count)], axis=1)
+
+
+def bucket_places(bucket, rows, starts_ref):
+    before = lax.broadcasted_iota(I32, (LANES, 2 * LANES), 0)
+    after = lax.broadcasted_iota(I32, (LANES, 2 * LANES), 1)
+    weights = jnp.where((before < after) | (after >= LANES), 1.0, 0.0).astype(BF16)
+    below = lax.broadcasted_iota(I32, (rows, rows), 0) > lax.broadcasted_iota(I32, (rows, rows), 1)
+    below = jnp.where(below, 1.0, 0.0).astype(BF16)
+    place = jnp.full((rows, LANES), -1.0, F32)
+    base = jnp.zeros((1, LANES), F32)
+    for b in range(BUCKETS):
+        starts_ref[b] = jnp.max(base).astype(I32)
+        here = bucket == b
+        counted = jnp.dot(
+            jnp.where(here, 1.0, 0.0).astype(BF16), weights, preferred_element_type=F32
+        )
+        totals = counted[:, LANES:]
+        offset = jnp.dot(below, totals.astype(BF16), preferred_element_type=F32)
+        place = jnp.where(here, counted[:, :LANES] + offset + base * float(BLOCK), place)
+        total = offset[rows - 1 :] + totals[rows - 1 :]
+        base = base + jnp.floor((total + (BLOCK - 1.0)) * (1.0 / BLOCK))
+    starts_ref[BUCKETS] = jnp.max(base).astype(I32)
+    return place
+
+
+def block_and_lane(place):
+    block = jnp.floor(place * (1.0 / BLOCK))
+    return block, place - block * float(BLOCK)
+
+
+def plan_kernel(
+    count_ref, owner_ref, cell_ref, area_ref, target_ref, order, starts, targets, facts, grid
+):
     live = count_ref[0]
     owners = lax.broadcasted_iota(I32, (DEVICES, RANK_BLOCK), 0)
     before = lax.broadcasted_iota(I32, (RANK_BLOCK, RANK_BLOCK), 0)
@@ -384,109 +450,151 @@
         ],
         axis=1,
     )
-    place = lax.broadcasted_iota(I32, (1, RANK_BLOCK), 1)
+    face = lax.broadcasted_iota(I32, (1, RANK_BLOCK), 1)
     base = jnp.zeros((DEVICES, RANK_BLOCK), F32)
     wide = RANK_BLOCK // LANES
     for block in range(FACES // RANK_BLOCK):
-        rows = [owner_ref[block * wide + i : block * wide + i + 1, :] for i in range(wide)]
-        named = jnp.concatenate(rows, axis=1)
-        is_live = place + block * RANK_BLOCK < live
-        named = jnp.where(is_live, named, -1)
+        named = lines(owner_ref, block * wide, wide)
+        named = jnp.where(face + block * RANK_BLOCK < live, named, -1)
         hits = jnp.where(owners == named, 1.0, 0.0)
         counted = jnp.dot(hits.astype(BF16), weights, preferred_element_type=F32)
         rank = jnp.sum(hits * (counted[:, :RANK_BLOCK] + base), axis=0, keepdims=True)
         base = base + counted[:, RANK_BLOCK:]
-        rank = jnp.where(is_live, rank.astype(I32), -1)
         for i in range(wide):
-            rank_out[block * wide + i : block * wide + i + 1, :] = rank[
+            facts[3, block * wide + i : block * wide + i + 1, :] = rank[
                 :, i * LANES : (i + 1) * LANES
             ]
 
-
-def ranks(counts, owner):
+    cell = cell_ref[...]
+    target = target_ref[...] + 1
+    row, column = cell >> 13, cell & (COLS - 1)
+    cell_row = row * TILES + ((column >> 7) & 7) * TILE + (column >> 10)
+    number = (
+        lax.broadcasted_iota(I32, (FACE_ROWS, LANES), 0) * LANES
+        + lax.broadcasted_iota(I32, (FACE_ROWS, LANES), 1)
+    )
+    bucket = jnp.where(number < live, cell_row >> 8, -1)
+    facts[0] = (cell_row & (BUCKET - 1)).astype(F32)
+    facts[1] = (column & (LANES - 1)).astype(F32)
+    facts[2] = jnp.where(number < live, owner_ref[...], -1).astype(F32)
+    facts[4], facts[5] = halves(area_ref[...] * (1.0 / SUBSTEPS))
+    for i in range(3):
+        facts[6 + i] = ((target >> (7 * i)) & (LANES - 1)).astype(F32)
+    facts[9], facts[10] = block_and_lane(bucket_places(bucket, FACE_ROWS, starts))
+
+    order[...] = jnp.zeros_like(order)
+    grid[...] = jnp.zeros_like(grid)
+    by_lane = indices(BLOCK, LINE)
+    by_block = indices(PLANNED, LINE)
+    by_device = indices(DEVICES, LINE)
+    wide = LINE // LANES
+
+    @pl.loop(0, FACES // LINE, unroll=2)
+    def _(step):
+        fact = [lines(facts.at[i], step * wide, wide) for i in range(11)]
+        order[...] += product(spread(by_block, fact[9], fact[:6]), one_hot(by_lane, fact[10]))
+        grid[...] += product(spread(by_device, fact[2], fact[6:9]), one_hot(by_device, fact[3]))
+
+    targets[...] = (
+        grid[:DEVICES]
+        + grid[DEVICES : 2 * DEVICES] * float(LANES)
+        + grid[2 * DEVICES :] * float(LANES * LANES)
+    )
+
+
+def plan(counts, owner, cell, area, target):
     return pl.pallas_call(
-        rank_kernel,
-        out_shape=jax.ShapeDtypeStruct((FACE_ROWS, LANES), I32),
-        in_specs=[SMEM, VMEM],
-        out_specs=VMEM,
+        plan_kernel,
+        out_shape=(
+            jax.ShapeDtypeStruct((6 * PLANNED, BLOCK), F32),
+            jax.ShapeDtypeStruct((BUCKETS + 1,), I32),
+            jax.ShapeDtypeStruct((DEVICES, RANKS), F32),
+        ),
+        in_specs=[SMEM] + [VMEM] * 4,
+        out_specs=(VMEM, SMEM, VMEM),
+        scratch_shapes=[
+            pltpu.VMEM((11, FACE_ROWS, LANES), F32),
+            pltpu.VMEM((3 * DEVICES, RANKS), F32),
+        ],
         compiler_params=params(),
-        name="ranks",
-    )(counts, owner)
-
-
-def halves(values):
-    high = values.astype(BF16).astype(F32)
-    return high, values - high
-
-
-PICK = 512
-
-
-def pick_kernel(total_ref, cell_ref, area_ref, owner_ref, target_ref, rank_ref, out, turned, slots):
+        name="plan",
+    )(counts, owner, cell, area, target)
+
+
+def bucket_of(block, starts_ref):
+    bucket = 0
+    for b in range(1, BUCKETS):
+        bucket = bucket + jnp.where(block >= starts_ref[b], 1, 0)
+    return bucket
+
+
+def steps_of(starts_ref):
+    return (starts_ref[BUCKETS] + TOGETHER - 1) // TOGETHER
+
+
+def pick_kernel(total_ref, order_ref, starts_ref, targets_ref, out, turned, slots):
     for part in range(3):
         for block in range(CELL_ROWS // LANES):
-            columns = slice(block * LANES, (block + 1) * LANES)
-            high, low = halves(total_ref[part, columns, :].T)
-            turned[2 * part * LANES : (2 * part + 1) * LANES, columns] = high.astype(BF16)
-            turned[(2 * part + 1) * LANES : (2 * part + 2) * LANES, columns] = low.astype(BF16)
+            high, low = halves(total_ref[part, block * LANES : (block + 1) * LANES, :].T)
+            bucket = block * LANES // BUCKET
+            columns = slice(block * LANES % BUCKET, block * LANES % BUCKET + LANES)
+            turned[bucket, 2 * part * LANES : (2 * part + 1) * LANES, columns] = high.astype(BF16)
+            turned[bucket, (2 * part + 1) * LANES : (2 * part + 2) * LANES, columns] = low.astype(
+                BF16
+            )
     slots[...] = jnp.zeros_like(slots)
-    wide = PICK // LANES
-    cell_rows = lax.broadcasted_iota(I32, (CELL_ROWS, PICK), 0)
-    index = lax.broadcasted_iota(I32, (LANES, PICK), 0)
-
-    @pl.loop(0, FACES // PICK)
-    def _(block):
-        def line(ref):
-            return jnp.concatenate([ref[pl.ds(block * wide + i, 1), :] for i in range(wide)], axis=1)
-
-        cell, area, owner, target, rank = (
-            line(ref) for ref in (cell_ref, area_ref, owner_ref, target_ref, rank_ref)
-        )
-        row, column = cell >> 13, cell & (COLS - 1)
-        cell_row = row * TILES + ((column >> 7) & 7) * TILE + (column >> 10)
-        picked = jnp.where(cell_rows == cell_row, 1.0, 0.0).astype(BF16)
-        found = jnp.dot(turned[...], picked, preferred_element_type=F32)
-        is_lane = index == (column & (LANES - 1))
-        is_rank = index == rank
-        parts = []
-        for part in range(3):
-            both = (
-                found[2 * part * LANES : (2 * part + 1) * LANES]
-                + found[(2 * part + 1) * LANES : (2 * part + 2) * LANES]
+    by_row = indices(BUCKET, BLOCK)
+    lane = lax.broadcasted_iota(I32, (LANES, BLOCK), 0).astype(F32)
+    by_device = indices(DEVICES, BLOCK * TOGETHER)
+
+    @pl.loop(0, steps_of(starts_ref))
+    def _(step):
+        surface = []
+        placed = []
+        for i in range(TOGETHER):
+            block = step * TOGETHER + i
+            row, where, owner, rank, high, low = (
+                order_ref[pl.ds(part * PLANNED + block, 1), :] for part in range(6)
             )
-            value = jnp.sum(jnp.where(is_lane, both, 0.0), axis=0, keepdims=True)
-            parts.extend(halves(value * (area * (1.0 / SUBSTEPS))))
-        for shift in (0, 7, 14):
-            parts.append(((target >> shift) & (LANES - 1)).astype(F32))
-        spread = jnp.concatenate(
-            [jnp.where(is_rank, part, 0.0).astype(BF16) for part in parts], axis=0
-        )
-        named = jnp.where(index == owner, 1.0, 0.0).astype(BF16)
-        slots[...] += lax.dot_general(
-            named, spread, (((1,), (1,)), ((), ())), preferred_element_type=F32
-        )
-
-    pieces = [slots[:, i * LANES : (i + 1) * LANES] for i in range(9)]
+            found = jnp.dot(
+                turned[bucket_of(block, starts_ref)],
+                one_hot(by_row, row),
+                preferred_element_type=F32,
+            )
+            is_lane = lane == where
+            parts = []
+            for part in range(3):
+                both = (
+                    found[2 * part * LANES : (2 * part + 1) * LANES]
+                    + found[(2 * part + 1) * LANES : (2 * part + 2) * LANES]
+                )
+                value = jnp.sum(jnp.where(is_lane, both, 0.0), axis=0, keepdims=True)
+                parts.extend(halves(value * (high + low)))
+            surface.append(parts)
+            placed.append((owner, rank))
+        joined = [jnp.concatenate(part, axis=1) for part in zip(*surface)]
+        owner, rank = (jnp.concatenate(part, axis=1) for part in zip(*placed))
+        slots[...] += product(spread(by_device, owner, joined), one_hot(by_device, rank))
+
+    pieces = [slots[i * DEVICES : (i + 1) * DEVICES] for i in range(6)]
     for part in range(3):
         out[pl.ds(part, DEVICES, stride=4), :] = pieces[2 * part] + pieces[2 * part + 1]
-    out[pl.ds(3, DEVICES, stride=4), :] = (
-        pieces[6] + pieces[7] * float(LANES) + pieces[8] * float(LANES * LANES)
-    )
-
-
-def pick(total, cell, area, owner, target, rank):
+    out[pl.ds(3, DEVICES, stride=4), :] = targets_ref[...]
+
+
+def pick(total, order, starts, targets):
     return pl.pallas_call(
         pick_kernel,
         out_shape=jax.ShapeDtypeStruct((4 * DEVICES, LANES), F32),
-        in_specs=[VMEM] * 6,
+        in_specs=[VMEM, VMEM, SMEM, VMEM],
         out_specs=VMEM,
         scratch_shapes=[
-            pltpu.VMEM((6 * LANES, CELL_ROWS), BF16),
-            pltpu.VMEM((DEVICES, 9 * LANES), F32),
+            pltpu.VMEM((BUCKETS, 6 * LANES, BUCKET), BF16),
+            pltpu.VMEM((6 * DEVICES, RANKS), F32),
         ],
         compiler_params=params(),
         name="pick",
-    )(total, cell, area, owner, target, rank)
+    )(total, order, starts, targets)
 
 
 def exchange_kernel(ready, arrived, local_sem, send_sem, recv_sem):
@@ -537,36 +645,39 @@
     )(ready)
 
 
-ADD = 512
-
-
-def add_kernel(arrived_ref, stepped_ref, out, held, sums):
-    for part in range(4):
-        held[part] = arrived_ref[pl.ds(part, DEVICES, stride=4), :]
+def add_kernel(arrived_ref, stepped_ref, out, held, order, sums, starts):
+    for part in range(3):
+        high, low = halves(arrived_ref[pl.ds(part, DEVICES, stride=4), :])
+        held[2 * part] = high
+        held[2 * part + 1] = low
+    target = arrived_ref[pl.ds(3, DEVICES, stride=4), :].astype(I32) - 1
+    row, column = target >> 13, target & (COLS - 1)
+    cell_row = ((row >> 3) * TILES + (column >> 7)) * TILE + (row & 7)
+    bucket = jnp.where(target >= 0, cell_row >> 8, -1)
+    held[6] = (cell_row & (BUCKET - 1)).astype(F32)
+    held[7] = (column & (LANES - 1)).astype(F32)
+    held[8], held[9] = block_and_lane(bucket_places(bucket, DEVICES, starts))
+    order[...] = jnp.zeros_like(order)
     sums[...] = jnp.zeros_like(sums)
-    wide = ADD // LANES
-    cell_rows = lax.broadcasted_iota(I32, (CELL_ROWS, ADD), 0)
-    index = lax.broadcasted_iota(I32, (LANES, ADD), 0)
-
-    @pl.loop(0, DEVICES * RANKS // ADD)
-    def _(block):
-        def line(part):
-            return jnp.concatenate(
-                [held[part, pl.ds(block * wide + i, 1), :] for i in range(wide)], axis=1
-            )
-
-        target = line(3).astype(I32)
-        row, column = target >> 13, target & (COLS - 1)
-        cell_row = ((row >> 3) * TILES + (column >> 7)) * TILE + (row & 7)
-        hits = jnp.where(cell_rows == cell_row, 1.0, 0.0).astype(BF16)
-        is_lane = index == (column & (LANES - 1))
-        parts = [half for part in range(3) for half in halves(line(part))]
-        spread = jnp.concatenate(
-            [jnp.where(is_lane, part, 0.0).astype(BF16) for part in parts], axis=0
-        )
-        sums[...] += lax.dot_general(
-            hits, spread, (((1,), (1,)), ((), ())), preferred_element_type=F32
-        )
+    by_lane = indices(BLOCK, LINE)
+    by_block = indices(SORTED, LINE)
+    wide = LINE // LANES
+
+    @pl.loop(0, DEVICES * RANKS // LINE, unroll=2)
+    def _(step):
+        fact = [lines(held.at[i], step * wide, wide) for i in range(10)]
+        order[...] += product(spread(by_block, fact[8], fact[:8]), one_hot(by_lane, fact[9]))
+
+    by_row = indices(BUCKET, BLOCK)
+    by_column = indices(LANES, BLOCK)
+
+    @pl.loop(0, steps_of(starts))
+    def _(step):
+        for i in range(TOGETHER):
+            block = step * TOGETHER + i
+            fact = [order[pl.ds(part * SORTED + block, 1), :] for part in range(8)]
+            bucket = bucket_of(block, starts)
+            sums[bucket] += product(one_hot(by_row, fact[6]), spread(by_column, fact[7], fact[:6]))
 
     for part in range(3):
         high = slice(2 * part * LANES, (2 * part + 1) * LANES)
@@ -575,9 +686,11 @@
             rows = slice(band * TILE, (band + 1) * TILE)
             for block in range(TILES):
                 first = (band * TILES + block) * TILE
+                bucket, first = first // BUCKET, first % BUCKET
                 columns = slice(block * LANES, (block + 1) * LANES)
                 out[part, rows, columns] = stepped_ref[part, rows, columns] + (
-                    sums[first : first + TILE, high] + sums[first : first + TILE, low]
+                    sums[bucket, first : first + TILE, high]
+                    + sums[bucket, first : first + TILE, low]
                 )
 
 
@@ -588,8 +701,10 @@
         in_specs=[VMEM] * 2,
         out_specs=VMEM,
         scratch_shapes=[
-            pltpu.VMEM((4, DEVICES, RANKS), F32),
-            pltpu.VMEM((CELL_ROWS, 6 * LANES), F32),
+            pltpu.VMEM((10, DEVICES, RANKS), F32),
+            pltpu.VMEM((8 * SORTED, BLOCK), F32),
+            pltpu.VMEM((BUCKETS, BUCKET, 6 * LANES), F32),
+            pltpu.SMEM((BUCKETS + 1,), I32),
         ],
         compiler_params=params(),
         name="add",
@@ -610,9 +725,9 @@
     cell, area, owner, target = (
         array.reshape(FACE_ROWS, LANES) for array in (face_cell, face_area, face_owner, face_target)
     )
-    rank = ranks(face_counts, owner)
+    order, starts, targets = plan(face_counts, owner, cell, area, target)
     les_final, total, stepped = fields(les_state[0], les_density[0], far_state[0], far_density[0])
-    ready = pick(total.reshape(3, CELL_ROWS, LANES), cell, area, owner, target, rank)
+    ready = pick(total.reshape(3, CELL_ROWS, LANES), order, starts, targets)
     arrived = exchange(ready.reshape(DEVICES, 4, LANES))
     far_final = add(arrived.reshape(4 * DEVICES, LANES), stepped)
     return les_final[None], far_final[None]

time: 153 us -> 123 us (0.80); the launches traced: 153 us -> 121 us
  Pallas kernels: 151 us -> 119 us
    pallas_call x1, Pallas kernels: 36.3 us -> 18.6 us  [add(): pl.pallas_call(add_kernel, out_shape=jax.ShapeDtypeStruct((3, ROWS, COLS)...]
    pallas_call x1, Pallas kernels: 25.8 us -> 9.77 us  [pick(): pl.pallas_call(pick_kernel, out_shape=jax.ShapeDtypeStruct((4 * DEVICES,...]
    pallas_call x1, Pallas kernels: 3.02 us -> 7.93 us  [plan(): pl.pallas_call(plan_kernel, out_shape=(jax.ShapeDtypeStruct((6 * PLANNED,...]
    pallas_call x1, Pallas kernels: 48.2 us -> 46.4 us  [fields(): pl.pallas_call(fields_kernel, out_shape=(block, jax.ShapeDtypeStruct((3,...]
where the time goes in v2:
time: 123 us; the launch traced here: 121 us
  Pallas kernels  119 us (97%)
  between operations  1.31 us (1%)
    pallas_call x1, Pallas kernels, fields(): pl.pallas_call(fields_kernel, out_shape=(block, jax.ShapeDtypeStruct((3,...  46.4 us
    pallas_call x1, Pallas kernels, exchange(): pl.pallas_call(exchange_kernel, out_shape=jax.ShapeDtypeStruct(ready.shap...  36.1 us
    pallas_call x1, Pallas kernels, add(): pl.pallas_call(add_kernel, out_shape=jax.ShapeDtypeStruct((3, ROWS, COLS)...  18.6 us
    pallas_call x1, Pallas kernels, pick(): pl.pallas_call(pick_kernel, out_shape=jax.ShapeDtypeStruct((4 * DEVICES,...  9.77 us
    pallas_call x1, Pallas kernels, plan(): pl.pallas_call(plan_kernel, out_shape=(jax.ShapeDtypeStruct((6 * PLANNED,...  7.93 us

profile of v2, /device:TPU:1, one launch (start us, length us, event | category | flops | bytes accessed | tf_op | source)
XLA Modules:
  0.0 121.2 jit_solution(16395444191669463016)
XLA Ops:
  0.6 46.4 %fields.1 = (f32[3,16,8192]{2,1,0:T(8,128)}, f32[3,16,64,128]{3,2,1,0:T(8,128)}, f32[3,16,8192]{2,1,0:T(8,128)}) custom-call(f32[3,16,8192]{2,1,0:T(8,128)} %bitcast.15, f32[16,8192]{1,0:T(8,128)} %bitcast.20, f32[3,16,8192]{2,1,0:T(8,128)} %bitcast.16, f32[16,8192]{1,0:T(8,128)} %bitcast.21), custom_call_target="tpu_custom_call" | custom-call | tf_op jit(solution)/shard_map/fields/pallas_call | solution.py:349
  47.6 7.9 %plan.1 = (f32[288,256]{1,0:T(8,128)}, s32[5]{0:T(128)}, f32[128,128]{1,0:T(8,128)}) custom-call(s32[1]{0:T(128)S(6)} %copy.12.count_ref, s32[64,128]{1,0:T(8,128)} %bitcast.22, s32[64,128]{1,0:T(8,128)} %bitcast.23, f32[64,128]{1,0:T(8,128)} %bitcast.24, s32[64,128]{1,0:T(8,128)} %bitcast.25), custom_call_target="tpu_custom_call" | custom-call | tf_op jit(solution)/shard_map/plan/pallas_call | solution.py:506
  55.6 9.8 %pick.1 = f32[512,128]{1,0:T(8,128)} custom-call(f32[3,1024,128]{2,1,0:T(8,128)} %bitcast.14, f32[288,256]{1,0:T(8,128)} %get-tuple-element.10.order_ref, s32[5]{0:T(128)} %get-tuple-element.11.starts_ref, f32[128,128]{1,0:T(8,128)} %get-tuple-element.12.targets_ref), custom_call_target="tpu_custom_call" | custom-call | tf_op jit(solution)/shard_map/pick/pallas_call | solution.py:586
  65.3 36.1 %exchange.1 = f32[128,4,128]{2,1,0:T(4,128)} custom-call(f32[128,4,128]{2,1,0:T(4,128)} %bitcast.18), custom_call_target="tpu_custom_call" | custom-call | tf_op jit(solution)/shard_map/exchange/pallas_call | solution.py:637
  101.5 0.0 copy-start
  101.5 18.6 %add.1 = f32[3,16,8192]{2,1,0:T(8,128)} custom-call(f32[512,128]{1,0:T(8,128)} %bitcast.19, f32[3,16,8192]{2,1,0:T(8,128)} %get-tuple-element.13.stepped_ref), custom_call_target="tpu_custom_call" | custom-call | tf_op jit(solution)/shard_map/add/pallas_call | solution.py:698
  120.1 0.0 copy-done
  120.1 1.1 copy.13
Async XLA Ops:
  101.5 18.6 %copy-start = (f32[3,16,8192]{2,1,0:T(8,128)S(1)}, f32[3,16,8192]{2,1,0:T(8,128)}, u32[]{:S(2)}) copy-start(f32[3,16,8192]{2,1,0:T(8,128)} %get-tuple-element.8) | copy-start | bytes 4718596

commit v3 on v2

--- a/solution.py
+++ b/solution.py
@@ -125,19 +125,23 @@
             device_id_type=MESH,
         )
 
-    def up_copy(sub):
-        sems = (send_sem.at[sub, 0], recv_sem.at[sub, 0])
-        return remote(state.at[sub], 3, 3, ROWS + 3, sems, up)
-
-    def down_copy(sub):
-        sems = (send_sem.at[sub, 1], recv_sem.at[sub, 1])
-        return remote(state.at[sub], ROWS, 3, 0, sems, down)
+    def up_copy(number):
+        sems = (send_sem.at[number, 0], recv_sem.at[number, 0])
+        near = number == 0
+        first, landing = (6, ROWS + 6) if near else (9, ROWS + 9)
+        return remote(state.at[0 if near else number - 1], first, 3, landing, sems, up)
+
+    def down_copy(number):
+        sems = (send_sem.at[number, 1], recv_sem.at[number, 1])
+        near = number == 0
+        first, landing = (ROWS + 3, 3) if near else (ROWS, 0)
+        return remote(state.at[0 if near else number - 1], first, 3, landing, sems, down)
 
     def inverse_up():
-        return remote(inverse, 1, 1, ROWS + 1, (inverse_send.at[0], inverse_recv.at[0]), up)
+        return remote(inverse, 4, 4, ROWS + 4, (inverse_send.at[0], inverse_recv.at[0]), up)
 
     def inverse_down():
-        return remote(inverse, ROWS, 1, 0, (inverse_send.at[1], inverse_recv.at[1]), down)
+        return remote(inverse, ROWS, 4, 0, (inverse_send.at[1], inverse_recv.at[1]), down)
 
     def far_up():
         return remote(far, 2, 2, ROWS + 2, (far_send.at[0], far_recv.at[0]), up)
@@ -148,15 +152,15 @@
     @pl.when(jnp.logical_not(has_up))
     def _():
         for sub in range(SUBSTEPS):
-            state[sub, 0:3] = jnp.zeros((3, 3, TILES, LANES), F32)
-        inverse[0] = jnp.zeros((TILES, LANES), F32)
+            state[sub, 0:6] = jnp.zeros((6, 3, TILES, LANES), F32)
+        advanced[0:4] = jnp.zeros((4, 3, TILES, LANES), F32)
         far[0:2] = jnp.zeros((2, 3, TILES, LANES), F32)
 
     @pl.when(jnp.logical_not(has_down))
     def _():
         for sub in range(SUBSTEPS):
-            state[sub, ROWS + 3 :] = jnp.zeros((3, 3, TILES, LANES), F32)
-        inverse[ROWS + 1] = jnp.zeros((TILES, LANES), F32)
+            state[sub, ROWS + 6 :] = jnp.zeros((6, 3, TILES, LANES), F32)
+        advanced[ROWS + 4 :] = jnp.zeros((4, 3, TILES, LANES), F32)
         far[ROWS + 2 : ROWS + 4] = jnp.zeros((2, 3, TILES, LANES), F32)
 
     def convert_state(source, target, offset):
@@ -184,14 +188,14 @@
             rows_from_tiles(load, flat, store, rows8)
 
     def advance(sub, row):
-        base = row + 3
+        base = row + 6
         u, v, p = (state[sub, base, part] for part in range(3))
         dx = [
             difference(*(state[sub, base + by, part] for by in (-2, -1, 1, 2)))
             for part in range(3)
         ]
         dy = [across(field, lane) for field in (u, v, p)]
-        inv = inverse[row + 1]
+        inv = inverse[row + 4]
         rate_u = u * dx[0] + v * dy[0] + inv * dx[2]
         rate_v = u * dx[1] + v * dy[1] + inv * dy[2]
         rate_p = u * dx[2] + v * dy[2] + LES_STIFF * (dx[0] + dy[1])
@@ -199,19 +203,26 @@
 
     def put_advanced(row, fields):
         for part in range(3):
-            advanced[row + 1, part] = fields[part]
-
-    def smooth(sub, row):
+            advanced[row + 4, part] = fields[part]
+
+    def advance_rows(sub, low, high):
+        loop(low, high, lambda row: put_advanced(row, advance(sub, row)))
+
+    def smooth(sub, row, own):
         for part in range(3):
-            centre = advanced[row + 1, part]
-            lateral = advanced[row, part] + advanced[row + 2, part]
+            centre = advanced[row + 4, part]
+            lateral = advanced[row + 3, part] + advanced[row + 5, part]
             sides = shifted(centre, 1, lane) + shifted(centre, -1, lane)
             value = (1.0 - FILTER_WEIGHT) * centre + FILTER_WEIGHT / 4.0 * (lateral + sides)
-            state[sub + 1, row + 3, part] = value
-            if sub == 0:
-                total_out[part, row] = value
-            else:
-                total_out[part, row] += value
+            state[sub + 1, row + 6, part] = value
+            if own:
+                if sub == 0:
+                    total_out[part, row] = value
+                else:
+                    total_out[part, row] += value
+
+    def smooth_rows(sub, low, high, own=True):
+        loop(low, high, lambda row: smooth(sub, row, own))
 
     def far_row(row):
         base = row + 2
@@ -243,8 +254,8 @@
 
             tiles_from_rows(load, flat, store, rows8)
 
-    convert_state(les_ref, state.at[0], 3)
-    convert_density(les_density_ref, inverse, 1)
+    convert_state(les_ref, state.at[0], 6)
+    convert_density(les_density_ref, inverse, 4)
 
     pl.semaphore_wait(barrier, jnp.where(has_up, 1, 0) + jnp.where(has_down, 1, 0))
 
@@ -252,15 +263,38 @@
     def _():
         up_copy(0).start()
         inverse_up().start()
+        up_copy(1).start()
 
     @pl.when(has_down)
     def _():
         down_copy(0).start()
         inverse_down().start()
+        down_copy(1).start()
 
     for sub in range(SUBSTEPS):
-        loop(2, ROWS - 2, lambda row: put_advanced(row, advance(sub, row)))
-        loop(3, ROWS - 3, lambda row: smooth(sub, row))
+        advance_rows(sub, 2, ROWS - 2)
+        smooth_rows(sub, 3, ROWS - 3)
+
+        if sub + 2 < SUBSTEPS:
+
+            @pl.when(has_up)
+            def _():
+                up_copy(sub + 2).start()
+
+            @pl.when(has_down)
+            def _():
+                down_copy(sub + 2).start()
+
+        if sub + 2 == SUBSTEPS:
+
+            @pl.when(has_up)
+            def _():
+                far_up().start()
+
+            @pl.when(has_down)
+            def _():
+                far_down().start()
+
         if sub == 0:
             convert_state(far_ref, far, 2)
             convert_density(far_density_ref, far_inverse, 0)
@@ -269,48 +303,39 @@
 
         @pl.when(has_up)
         def _():
-            down_copy(sub).wait_recv()
             if sub == 0:
+                down_copy(0).wait_recv()
                 inverse_down().wait_recv()
-
-        loop(0, 2, lambda row: put_advanced(row, advance(sub, row)))
-        put_advanced(-1, [jnp.where(has_up, field, 0.0) for field in advance(sub, -1)])
-        loop(0, 3, lambda row: smooth(sub, row))
-
-        if sub < SUBSTEPS - 1:
+            put_advanced(-1, advance(sub, -1))
+
+        @pl.when(has_down)
+        def _():
+            if sub == 0:
+                up_copy(0).wait_recv()
+                inverse_up().wait_recv()
+            put_advanced(ROWS, advance(sub, ROWS))
+
+        advance_rows(sub, 0, 2)
+        advance_rows(sub, ROWS - 2, ROWS)
+        smooth_rows(sub, 0, 3)
+        smooth_rows(sub, ROWS - 3, ROWS)
+
+        if sub + 1 < SUBSTEPS:
 
             @pl.when(has_up)
             def _():
-                up_copy(sub + 1).start()
-
-        @pl.when(has_down)
-        def _():
-            up_copy(sub).wait_recv()
-            if sub == 0:
-                inverse_up().wait_recv()
-
-        loop(ROWS - 2, ROWS, lambda row: put_advanced(row, advance(sub, row)))
-        put_advanced(ROWS, [jnp.where(has_down, field, 0.0) for field in advance(sub, ROWS)])
-        loop(ROWS - 3, ROWS, lambda row: smooth(sub, row))
-
-        if sub < SUBSTEPS - 1:
+                down_copy(sub + 1).wait_recv()
+                advance_rows(sub, -4, -1)
+                smooth_rows(sub, -3, 0, own=False)
 
             @pl.when(has_down)
             def _():
-                down_copy(sub + 1).start()
-
-        if sub == SUBSTEPS - 2:
-
-            @pl.when(has_up)
-            def _():
-                far_up().start()
-
-            @pl.when(has_down)
-            def _():
-                far_down().start()
+                up_copy(sub + 1).wait_recv()
+                advance_rows(sub, ROWS + 1, ROWS + 4)
+                smooth_rows(sub, ROWS, ROWS + 3, own=False)
 
     write_tiles(
-        lambda row, part, reg: state[SUBSTEPS, row + 3, part, reg * TILE : (reg + 1) * TILE, :],
+        lambda row, part, reg: state[SUBSTEPS, row + 6, part, reg * TILE : (reg + 1) * TILE, :],
         les_out,
     )
 
@@ -352,9 +377,9 @@
         in_specs=[VMEM] * 4,
         out_specs=(VMEM,) * 3,
         scratch_shapes=[
-            pltpu.VMEM((SUBSTEPS + 1, ROWS + 6, 3, TILES, LANES), F32),
-            pltpu.VMEM((ROWS + 2, 3, TILES, LANES), F32),
-            pltpu.VMEM((ROWS + 2, TILES, LANES), F32),
+            pltpu.VMEM((SUBSTEPS + 1, ROWS + 12, 3, TILES, LANES), F32),
+            pltpu.VMEM((ROWS + 8, 3, TILES, LANES), F32),
+            pltpu.VMEM((ROWS + 8, TILES, LANES), F32),
             pltpu.VMEM((2 * ROWS + 6, 3, TILES, LANES), F32),
             pltpu.VMEM((ROWS, TILES, LANES), F32),
             pltpu.VMEM((TILES * TILE, LANES), F32),

time: 123 us -> 115 us (0.935); the launches traced: 121 us -> 114 us
  Pallas kernels: 119 us -> 112 us
    pallas_call x1, Pallas kernels: 36.1 us -> 28 us  [exchange(): pl.pallas_call(exchange_kernel, out_shape=jax.ShapeDtypeStruct(ready.shap...]
    pallas_call x1, Pallas kernels: 46.4 us -> 48.9 us  [fields(): pl.pallas_call(fields_kernel, out_shape=(block, jax.ShapeDtypeStruct((3,...]
    pallas_call x1, Pallas kernels: 9.77 us -> 7.76 us  [pick(): pl.pallas_call(pick_kernel, out_shape=jax.ShapeDtypeStruct((4 * DEVICES,...]
where the time goes in v3:
time: 115 us; the launch traced here: 114 us
  Pallas kernels  112 us (97%)
  between operations  1.31 us (1%)
    pallas_call x1, Pallas kernels, fields(): pl.pallas_call(fields_kernel, out_shape=(block, jax.ShapeDtypeStruct((3,...  48.9 us
    pallas_call x1, Pallas kernels, exchange(): pl.pallas_call(exchange_kernel, out_shape=jax.ShapeDtypeStruct(ready.shap...  28 us
    pallas_call x1, Pallas kernels, add(): pl.pallas_call(add_kernel, out_shape=jax.ShapeDtypeStruct((3, ROWS, COLS)...  19.4 us
    pallas_call x1, Pallas kernels, plan(): pl.pallas_call(plan_kernel, out_shape=(jax.ShapeDtypeStruct((6 * PLANNED,...  7.94 us
    pallas_call x1, Pallas kernels, pick(): pl.pallas_call(pick_kernel, out_shape=jax.ShapeDtypeStruct((4 * DEVICES,...  7.76 us

profile of v3, /device:TPU:1, one launch (start us, length us, event | category | flops | bytes accessed | tf_op | source)
XLA Modules:
  0.0 114.5 jit_solution(16460405969084307832)
XLA Ops:
  0.6 48.9 %fields.1 = (f32[3,16,8192]{2,1,0:T(8,128)}, f32[3,16,64,128]{3,2,1,0:T(8,128)}, f32[3,16,8192]{2,1,0:T(8,128)}) custom-call(f32[3,16,8192]{2,1,0:T(8,128)} %bitcast.15, f32[16,8192]{1,0:T(8,128)} %bitcast.20, f32[3,16,8192]{2,1,0:T(8,128)} %bitcast.16, f32[16,8192]{1,0:T(8,128)} %bitcast.21), custom_call_target="tpu_custom_call" | custom-call | tf_op jit(solution)/shard_map/fields/pallas_call | solution.py:374
  50.2 7.9 %plan.1 = (f32[288,256]{1,0:T(8,128)}, s32[5]{0:T(128)}, f32[128,128]{1,0:T(8,128)}) custom-call(s32[1]{0:T(128)S(6)} %copy.12.count_ref, s32[64,128]{1,0:T(8,128)} %bitcast.22, s32[64,128]{1,0:T(8,128)} %bitcast.23, f32[64,128]{1,0:T(8,128)} %bitcast.24, s32[64,128]{1,0:T(8,128)} %bitcast.25), custom_call_target="tpu_custom_call" | custom-call | tf_op jit(solution)/shard_map/plan/pallas_call | solution.py:531
  58.1 7.8 %pick.1 = f32[512,128]{1,0:T(8,128)} custom-call(f32[3,1024,128]{2,1,0:T(8,128)} %bitcast.14, f32[288,256]{1,0:T(8,128)} %get-tuple-element.10.order_ref, s32[5]{0:T(128)} %get-tuple-element.11.starts_ref, f32[128,128]{1,0:T(8,128)} %get-tuple-element.12.targets_ref), custom_call_target="tpu_custom_call" | custom-call | tf_op jit(solution)/shard_map/pick/pallas_call | solution.py:611
  65.9 28.0 %exchange.1 = f32[128,4,128]{2,1,0:T(4,128)} custom-call(f32[128,4,128]{2,1,0:T(4,128)} %bitcast.18), custom_call_target="tpu_custom_call" | custom-call | tf_op jit(solution)/shard_map/exchange/pallas_call | solution.py:662
  93.9 0.0 copy-start
  93.9 19.4 %add.1 = f32[3,16,8192]{2,1,0:T(8,128)} custom-call(f32[512,128]{1,0:T(8,128)} %bitcast.19, f32[3,16,8192]{2,1,0:T(8,128)} %get-tuple-element.13.stepped_ref), custom_call_target="tpu_custom_call" | custom-call | tf_op jit(solution)/shard_map/add/pallas_call | solution.py:723
  113.3 0.0 copy-done
  113.4 1.1 copy.13
Async XLA Ops:
  93.9 19.4 %copy-start = (f32[3,16,8192]{2,1,0:T(8,128)S(1)}, f32[3,16,8192]{2,1,0:T(8,128)}, u32[]{:S(2)}) copy-start(f32[3,16,8192]{2,1,0:T(8,128)} %get-tuple-element.8) | copy-start | bytes 4718596

commit v4 on v3

v4 whole, which is shorter than its diff:
```python
import jax
import jax.numpy as jnp
from jax import lax
from jax.experimental import pallas as pl
from jax.experimental.pallas import tpu as pltpu
from jax.sharding import PartitionSpec as P

SUBSTEPS = 5
UNROLL = {12: 4, 10: 5}
TIME_STEP = 0.1
LES_STIFF = 1.0
FAR_STIFF = 1.0
FILTER_WEIGHT = 0.5
MEAN_FLOW = 0.3

LANES = 128
TILE = 8
ROWS = 16
COLS = 8192
TILES = COLS // LANES
REGS = TILES // TILE
FACES = 8192
FACE_ROWS = FACES // LANES
DEVICES = 128
RANKS = 128
CELL_ROWS = ROWS * COLS // LANES

MESH = pl.DeviceIdType.MESH
VMEM = pl.BlockSpec(memory_space=pltpu.VMEM)
SMEM = pl.BlockSpec(memory_space=pltpu.SMEM)
F32 = jnp.float32
BF16 = jnp.bfloat16
I32 = jnp.int32


def params(**more):
    return pltpu.CompilerParams(vmem_limit_bytes=56 * 1024 * 1024, **more)


def rows_from_tiles(load, flat, store, rows8):
    for block in range(TILES):
        flat[block * TILE : (block + 1) * TILE, :] = load(block)
    for row in range(TILE):
        for reg in range(REGS):
            store(rows8 * TILE + row, reg, flat[pl.ds(TILE * reg + row, TILE, stride=TILES), :])


def tiles_from_rows(load, flat, store, rows8):
    for row in range(TILE):
        for reg in range(REGS):
            flat[pl.ds(TILE * reg + row, TILE, stride=TILES), :] = load(rows8 * TILE + row, reg)
    for block in range(TILES):
        store(block, flat[block * TILE : (block + 1) * TILE, :])


def shifted(row, by, lane):
    if by > 0:
        turned = pltpu.roll(row, LANES - by, 1)
        crossed = jnp.concatenate([turned[TILE:], pltpu.roll(turned[:TILE], TILE - 1, 0)], axis=0)
        return jnp.where(lane >= LANES - by, crossed, turned)
    turned = pltpu.roll(row, -by, 1)
    crossed = jnp.concatenate(
        [pltpu.roll(turned[TILES - TILE :], 1, 0), turned[: TILES - TILE]], axis=0
    )
    return jnp.where(lane < -by, crossed, turned)


def difference(far_left, left, right, far_right):
    return 8.0 * (right - left) - (far_right - far_left)


def across(row, lane):
    return difference(
        shifted(row, -2, lane), shifted(row, -1, lane), shifted(row, 1, lane), shifted(row, 2, lane)
    )


RANK_BLOCK = 256
BUCKETS = 4
BUCKET = CELL_ROWS // BUCKETS
BLOCK = 256
LINE = 512
TOGETHER = 4
HALF = DEVICES // 2
PLANNED = 48
SORTED = 80


def halves(values):
    high = values.astype(BF16).astype(F32)
    return high, values - high


def indices(rows, columns):
    return lax.broadcasted_iota(I32, (rows, columns), 0).astype(F32).astype(BF16)


def one_hot(index, line):
    return jnp.where(index == line.astype(BF16), jnp.ones((), BF16), jnp.zeros((), BF16))


def spread(index, line, parts):
    here = index == line.astype(BF16)
    return jnp.concatenate(
        [jnp.where(here, part.astype(BF16), jnp.zeros((), BF16)) for part in parts], axis=0
    )


def product(left, right):
    return lax.dot_general(left, right, (((1,), (1,)), ((), ())), preferred_element_type=F32)


def lines(ref, first, count):
    return jnp.concatenate([ref[pl.ds(first + i, 1), :] for i in range(count)], axis=1)


def bucket_places(bucket, rows, starts_ref):
    before = lax.broadcasted_iota(I32, (LANES, 2 * LANES), 0)
    after = lax.broadcasted_iota(I32, (LANES, 2 * LANES), 1)
    weights = jnp.where((before < after) | (after >= LANES), 1.0, 0.0).astype(BF16)
    below = lax.broadcasted_iota(I32, (rows, rows), 0) > lax.broadcasted_iota(I32, (rows, rows), 1)
    below = jnp.where(below, 1.0, 0.0).astype(BF16)
    place = jnp.full((rows, LANES), -1.0, F32)
    base = jnp.zeros((1, LANES), F32)
    for b in range(BUCKETS):
        starts_ref[b] = jnp.max(base).astype(I32)
        here = bucket == b
        counted = jnp.dot(
            jnp.where(here, 1.0, 0.0).astype(BF16), weights, preferred_element_type=F32
        )
        totals = counted[:, LANES:]
        offset = jnp.dot(below, totals.astype(BF16), preferred_element_type=F32)
        place = jnp.where(here, counted[:, :LANES] + offset + base * float(BLOCK), place)
        total = offset[rows - 1 :] + totals[rows - 1 :]
        base = base + jnp.floor((total + (BLOCK - 1.0)) * (1.0 / BLOCK))
    starts_ref[BUCKETS] = jnp.max(base).astype(I32)
    return place


def block_and_lane(place):
    block = jnp.floor(place * (1.0 / BLOCK))
    return block, place - block * float(BLOCK)


def by_owner(halved):
    return jnp.concatenate([halved[:, :RANKS], halved[:, RANKS:]], axis=0)


def bucket_of(block, starts_ref):
    bucket = 0
    for b in range(1, BUCKETS):
        bucket = bucket + jnp.where(block >= starts_ref[b], 1, 0)
    return bucket


def steps_of(starts_ref):
    return (starts_ref[BUCKETS] + TOGETHER - 1) // TOGETHER


def rank_faces(count_ref, owner_ref, facts):
    live = count_ref[0]
    owners = lax.broadcasted_iota(I32, (DEVICES, RANK_BLOCK), 0)
    before = lax.broadcasted_iota(I32, (RANK_BLOCK, RANK_BLOCK), 0)
    after = lax.broadcasted_iota(I32, (RANK_BLOCK, RANK_BLOCK), 1)
    weights = jnp.concatenate(
        [
            jnp.where(before < after, 1.0, 0.0).astype(BF16),
            jnp.ones((RANK_BLOCK, RANK_BLOCK), BF16),
        ],
        axis=1,
    )
    face = lax.broadcasted_iota(I32, (1, RANK_BLOCK), 1)
    base = jnp.zeros((DEVICES, RANK_BLOCK), F32)
    wide = RANK_BLOCK // LANES
    for block in range(FACES // RANK_BLOCK):
        named = lines(owner_ref, block * wide, wide)
        named = jnp.where(face + block * RANK_BLOCK < live, named, -1)
        hits = jnp.where(owners == named, 1.0, 0.0)
        counted = jnp.dot(hits.astype(BF16), weights, preferred_element_type=F32)
        rank = jnp.sum(hits * (counted[:, :RANK_BLOCK] + base), axis=0, keepdims=True)
        base = base + counted[:, RANK_BLOCK:]
        for i in range(wide):
            facts[3, block * wide + i : block * wide + i + 1, :] = rank[
                :, i * LANES : (i + 1) * LANES
            ]


def sort_faces(
    count_ref, owner_ref, cell_ref, area_ref, target_ref, order, starts, targets, facts, grid
):
    live = count_ref[0]
    cell = cell_ref[...]
    target = target_ref[...] + 1
    row, column = cell >> 13, cell & (COLS - 1)
    cell_row = row * TILES + ((column >> 7) & 7) * TILE + (column >> 10)
    number = (
        lax.broadcasted_iota(I32, (FACE_ROWS, LANES), 0) * LANES
        + lax.broadcasted_iota(I32, (FACE_ROWS, LANES), 1)
    )
    bucket = jnp.where(number < live, cell_row >> 8, -1)
    facts[0] = (cell_row & (BUCKET - 1)).astype(F32)
    facts[1] = (column & (LANES - 1)).astype(F32)
    owner = owner_ref[...]
    facts[2] = jnp.where(number < live, owner & (HALF - 1), -1).astype(F32)
    facts[3] = facts[3] + ((owner >> 6) * RANKS).astype(F32)
    facts[4], facts[5] = halves(area_ref[...] * (1.0 / SUBSTEPS))
    for i in range(3):
        facts[6 + i] = ((target >> (7 * i)) & (LANES - 1)).astype(F32)
    facts[9], facts[10] = block_and_lane(bucket_places(bucket, FACE_ROWS, starts))

    order[...] = jnp.zeros_like(order)
    grid[...] = jnp.zeros_like(grid)
    by_lane = indices(BLOCK, LINE)
    by_block = indices(PLANNED, LINE)
    by_half = indices(HALF, LINE)
    wide = LINE // LANES

    @pl.loop(0, FACES // LINE, unroll=2)
    def _(step):
        fact = [lines(facts.at[i], step * wide, wide) for i in range(11)]
        order[...] += product(spread(by_block, fact[9], fact[:6]), one_hot(by_lane, fact[10]))
        grid[...] += product(spread(by_half, fact[2], fact[6:9]), one_hot(by_lane, fact[3]))

    targets[...] = by_owner(
        grid[:HALF]
        + grid[HALF : 2 * HALF] * float(LANES)
        + grid[2 * HALF :] * float(LANES * LANES)
    )


def pick_faces(total_ref, order_ref, starts_ref, targets_ref, ready, turned, slots):
    for part in range(3):
        for block in range(CELL_ROWS // LANES):
            high, low = halves(total_ref[part, 2 * block : 2 * block + 2].reshape(LANES, LANES).T)
            bucket = block * LANES // BUCKET
            columns = slice(block * LANES % BUCKET, block * LANES % BUCKET + LANES)
            turned[bucket, 2 * part * LANES : (2 * part + 1) * LANES, columns] = high.astype(BF16)
            turned[bucket, (2 * part + 1) * LANES : (2 * part + 2) * LANES, columns] = low.astype(
                BF16
            )
    slots[...] = jnp.zeros_like(slots)
    by_row = indices(BUCKET, BLOCK)
    lane = lax.broadcasted_iota(I32, (LANES, BLOCK), 0).astype(F32)
    by_half = indices(HALF, BLOCK * TOGETHER)
    by_rank = indices(2 * RANKS, BLOCK * TOGETHER)

    @pl.loop(0, (FACES // BLOCK + BUCKETS) // TOGETHER)
    def _(step):
        surface = []
        placed = []
        for i in range(TOGETHER):
            block = step * TOGETHER + i
            row, where, owner, rank, high, low = (
                order_ref[pl.ds(part * PLANNED + block, 1), :] for part in range(6)
            )
            found = jnp.dot(
                turned[bucket_of(block, starts_ref)],
                one_hot(by_row, row),
                preferred_element_type=F32,
            )
            is_lane = lane == where
            parts = []
            for part in range(3):
                both = (
                    found[2 * part * LANES : (2 * part + 1) * LANES]
                    + found[(2 * part + 1) * LANES : (2 * part + 2) * LANES]
                )
                value = jnp.sum(jnp.where(is_lane, both, 0.0), axis=0, keepdims=True)
                parts.extend(halves(value * (high + low)))
            surface.append(parts)
            placed.append((owner, rank))
        joined = [jnp.concatenate(part, axis=1) for part in zip(*surface)]
        owner, rank = (jnp.concatenate(part, axis=1) for part in zip(*placed))
        slots[...] += product(spread(by_half, owner, joined), one_hot(by_rank, rank))

    for part in range(3):
        first = 2 * part * HALF
        ready[:, part, :] = by_owner(
            slots[first : first + HALF] + slots[first + HALF : first + 2 * HALF]
        )
    ready[:, 3, :] = targets_ref[...]


def fields_kernel(
    les_ref,
    les_density_ref,
    far_ref,
    far_density_ref,
    count_ref,
    owner_ref,
    cell_ref,
    area_ref,
    target_ref,
    les_out,
    stepped_out,
    arrived,
    total_out,
    state,
    advanced,
    inverse,
    far,
    far_inverse,
    flat,
    send_sem,
    recv_sem,
    inverse_send,
    inverse_recv,
    far_send,
    far_recv,
    order,
    starts,
    targets,
    facts,
    grid,
    ready,
    turned,
    slots,
    local_sem,
    faces_send,
    faces_recv,
):
    dom = lax.axis_index("dom")
    doms = lax.axis_size("dom")
    has_up = dom > 0
    has_down = dom < doms - 1
    up = lax.rem(dom + doms - 1, doms)
    down = lax.rem(dom + 1, doms)
    lane = lax.broadcasted_iota(I32, (TILES, LANES), 1)
    step = TIME_STEP / 12.0

    devices = lax.axis_size("sec") * doms
    me = lax.axis_index("sec") * doms + dom
    barrier = pltpu.get_barrier_semaphore()

    def place(offset):
        other = lax.rem(me + offset, devices)
        return other, {"sec": other // doms, "dom": lax.rem(other, doms)}

    @pl.loop(1, devices)
    def _(offset):
        pl.semaphore_signal(barrier, inc=1, device_id=place(offset)[1], device_id_type=MESH)

    def remote(ref, first, count, landing, sems, where):
        return pltpu.make_async_remote_copy(
            src_ref=ref.at[pl.ds(first, count)],
            dst_ref=ref.at[pl.ds(landing, count)],
            send_sem=sems[0],
            recv_sem=sems[1],
            device_id={"dom": where},
            device_id_type=MESH,
        )

    def up_copy(number):
        sems = (send_sem.at[number, 0], recv_sem.at[number, 0])
        near = number == 0
        first, landing = (6, ROWS + 6) if near else (9, ROWS + 9)
        return remote(state.at[0 if near else number - 1], first, 3, landing, sems, up)

    def down_copy(number):
        sems = (send_sem.at[number, 1], recv_sem.at[number, 1])
        near = number == 0
        first, landing = (ROWS + 3, 3) if near else (ROWS, 0)
        return remote(state.at[0 if near else number - 1], first, 3, landing, sems, down)

    def inverse_up():
        return remote(inverse, 4, 4, ROWS + 4, (inverse_send.at[0], inverse_recv.at[0]), up)

    def inverse_down():
        return remote(inverse, ROWS, 4, 0, (inverse_send.at[1], inverse_recv.at[1]), down)

    def far_up():
        return remote(far, 2, 2, ROWS + 2, (far_send.at[0], far_recv.at[0]), up)

    def far_down():
        return remote(far, ROWS, 2, 0, (far_send.at[1], far_recv.at[1]), down)

    @pl.when(jnp.logical_not(has_up))
    def _():
        for sub in range(SUBSTEPS):
            state[sub, 0:6] = jnp.zeros((6, 3, TILES, LANES), F32)
        advanced[0:4] = jnp.zeros((4, 3, TILES, LANES), F32)
        far[0:2] = jnp.zeros((2, 3, TILES, LANES), F32)

    @pl.when(jnp.logical_not(has_down))
    def _():
        for sub in range(SUBSTEPS):
            state[sub, ROWS + 6 :] = jnp.zeros((6, 3, TILES, LANES), F32)
        advanced[ROWS + 4 :] = jnp.zeros((4, 3, TILES, LANES), F32)
        far[ROWS + 2 : ROWS + 4] = jnp.zeros((2, 3, TILES, LANES), F32)

    def convert_state(source, target, offset):
        @pl.loop(0, 6)
        def _(index):
            part, rows8 = index // 2, index % 2

            def load(block):
                return source[part, pl.ds(rows8 * TILE, TILE), block * LANES : (block + 1) * LANES]

            def store(row, reg, value):
                target[offset + row, part, reg * TILE : (reg + 1) * TILE, :] = value

            rows_from_tiles(load, flat, store, rows8)

    def convert_density(source, target, offset):
        @pl.loop(0, 2)
        def _(rows8):
            def load(block):
                return 1.0 / source[pl.ds(rows8 * TILE, TILE), block * LANES : (block + 1) * LANES]

            def store(row, reg, value):
                target[offset + row, reg * TILE : (reg + 1) * TILE, :] = value

            rows_from_tiles(load, flat, store, rows8)

    def advance(sub, row):
        base = row + 6
        u, v, p = (state[sub, base, part] for part in range(3))
        dx = [
            difference(*(state[sub, base + by, part] for by in (-2, -1, 1, 2)))
            for part in range(3)
        ]
        dy = [across(field, lane) for field in (u, v, p)]
        inv = inverse[row + 4]
        rate_u = u * dx[0] + v * dy[0] + inv * dx[2]
        rate_v = u * dx[1] + v * dy[1] + inv * dy[2]
        rate_p = u * dx[2] + v * dy[2] + LES_STIFF * (dx[0] + dy[1])
        return u - step * rate_u, v - step * rate_v, p - step * rate_p

    def put_advanced(row, fields):
        for part in range(3):
            advanced[row + 4, part] = fields[part]

    def advance_rows(sub, low, high):
        loop(low, high, lambda row: put_advanced(row, advance(sub, row)))

    def smooth(sub, row, own):
        for part in range(3):
            centre = advanced[row + 4, part]
            lateral = advanced[row + 3, part] + advanced[row + 5, part]
            sides = shifted(centre, 1, lane) + shifted(centre, -1, lane)
            value = (1.0 - FILTER_WEIGHT) * centre + FILTER_WEIGHT / 4.0 * (lateral + sides)
            state[sub + 1, row + 6, part] = value
            if own:
                if sub == 0:
                    total_out[part, row] = value
                else:
                    total_out[part, row] += value

    def smooth_rows(sub, low, high, own=True):
        loop(low, high, lambda row: smooth(sub, row, own))

    def far_row(row):
        base = row + 2
        u, v, p = (far[base, part] for part in range(3))
        dx = [
            difference(*(far[base + by, part] for by in (-2, -1, 1, 2))) for part in range(3)
        ]
        inv = far_inverse[row]
        dy_v, dy_p = across(v, lane), across(p, lane)
        far[base + ROWS + 4, 0] = u - step * (MEAN_FLOW * dx[0] + inv * dx[2])
        far[base + ROWS + 4, 1] = v - step * (MEAN_FLOW * dx[1] + inv * dy_p)
        far[base + ROWS + 4, 2] = p - step * (MEAN_FLOW * dx[2] + FAR_STIFF * (dx[0] + dy_v))

    def loop(low, high, body):
        @pl.loop(low, high, unroll=UNROLL.get(high - low, high - low))
        def _(row):
            body(row)

    def write_tiles(source, target):
        @pl.loop(0, 6)
        def _(index):
            part, rows8 = index // 2, index % 2

            def load(row, reg):
                return source(row, part, reg)

            def store(block, value):
                target[part, pl.ds(rows8 * TILE, TILE), block * LANES : (block + 1) * LANES] = value

            tiles_from_rows(load, flat, store, rows8)

    convert_state(les_ref, state.at[0], 6)
    convert_density(les_density_ref, inverse, 4)

    pl.semaphore_wait(barrier, devices - 1)

    @pl.when(has_up)
    def _():
        up_copy(0).start()
        inverse_up().start()
        up_copy(1).start()

    @pl.when(has_down)
    def _():
        down_copy(0).start()
        inverse_down().start()
        down_copy(1).start()

    for sub in range(SUBSTEPS):
        advance_rows(sub, 2, ROWS - 2)
        smooth_rows(sub, 3, ROWS - 3)

        if sub + 2 < SUBSTEPS:

            @pl.when(has_up)
            def _():
                up_copy(sub + 2).start()

            @pl.when(has_down)
            def _():
                down_copy(sub + 2).start()

        if sub + 2 == SUBSTEPS:

            @pl.when(has_up)
            def _():
                far_up().start()

            @pl.when(has_down)
            def _():
                far_down().start()

        if sub == 0:
            convert_state(far_ref, far, 2)
            convert_density(far_density_ref, far_inverse, 0)
            rank_faces(count_ref, owner_ref, facts)
        if sub == 1:
            sort_faces(
                count_ref,
                owner_ref,
                cell_ref,
                area_ref,
                target_ref,
                order,
                starts,
                targets,
                facts,
                grid,
            )
        if sub == 2:
            loop(2, ROWS - 2, far_row)

        @pl.when(has_up)
        def _():
            if sub == 0:
                down_copy(0).wait_recv()
                inverse_down().wait_recv()
            put_advanced(-1, advance(sub, -1))

        @pl.when(has_down)
        def _():
            if sub == 0:
                up_copy(0).wait_recv()
                inverse_up().wait_recv()
            put_advanced(ROWS, advance(sub, ROWS))

        advance_rows(sub, 0, 2)
        advance_rows(sub, ROWS - 2, ROWS)
        smooth_rows(sub, 0, 3)
        smooth_rows(sub, ROWS - 3, ROWS)

        if sub + 1 < SUBSTEPS:

            @pl.when(has_up)
            def _():
                down_copy(sub + 1).wait_recv()
                advance_rows(sub, -4, -1)
                smooth_rows(sub, -3, 0, own=False)

            @pl.when(has_down)
            def _():
                up_copy(sub + 1).wait_recv()
                advance_rows(sub, ROWS + 1, ROWS + 4)
                smooth_rows(sub, ROWS, ROWS + 3, own=False)

    pick_faces(total_out, order, starts, targets, ready, turned, slots)
    own = pltpu.make_async_copy(ready.at[me], arrived.at[me], local_sem)
    own.start()

    @pl.loop(1, devices)
    def _(offset):
        other, where = place(offset)
        pltpu.make_async_remote_copy(
            src_ref=ready.at[other],
            dst_ref=arrived.at[me],
            send_sem=faces_send,
            recv_sem=faces_recv,
            device_id=where,
            device_id_type=MESH,
        ).start()

    write_tiles(
        lambda row, part, reg: state[SUBSTEPS, row + 6, part, reg * TILE : (reg + 1) * TILE, :],
        les_out,
    )

    @pl.when(has_up)
    def _():
        far_down().wait_recv()

    @pl.when(has_down)
    def _():
        far_up().wait_recv()

    loop(0, 2, far_row)
    loop(ROWS - 2, ROWS, far_row)
    write_tiles(
        lambda row, part, reg: far[row + ROWS + 6, part, reg * TILE : (reg + 1) * TILE, :],
        stepped_out,
    )

    @pl.when(has_up)
    def _():
        for sub in range(SUBSTEPS):
            up_copy(sub).wait_send()
        inverse_up().wait_send()
        far_up().wait_send()

    @pl.when(has_down)
    def _():
        for sub in range(SUBSTEPS):
            down_copy(sub).wait_send()
        inverse_down().wait_send()
        far_down().wait_send()

    own.wait()
    all_but_one = pl.ds(0, devices - 1)
    pltpu.make_async_copy(arrived.at[all_but_one], arrived.at[all_but_one], faces_recv).wait()
    pltpu.make_async_copy(ready.at[all_but_one], ready.at[all_but_one], faces_send).wait()


def fields(les_state, les_density, far_state, far_density, counts, owner, cell, area, target):
    block = jax.ShapeDtypeStruct((3, ROWS, COLS), F32)
    dma = pltpu.SemaphoreType.DMA
    return pl.pallas_call(
        fields_kernel,
        out_shape=(block, block, jax.ShapeDtypeStruct((DEVICES, 4, RANKS), F32)),
        in_specs=[VMEM] * 4 + [SMEM] + [VMEM] * 4,
        out_specs=(VMEM,) * 3,
        scratch_shapes=[
            pltpu.VMEM((3, ROWS, TILES, LANES), F32),
            pltpu.VMEM((SUBSTEPS + 1, ROWS + 12, 3, TILES, LANES), F32),
            pltpu.VMEM((ROWS + 8, 3, TILES, LANES), F32),
            pltpu.VMEM((ROWS + 8, TILES, LANES), F32),
            pltpu.VMEM((2 * ROWS + 6, 3, TILES, LANES), F32),
            pltpu.VMEM((ROWS, TILES, LANES), F32),
            pltpu.VMEM((TILES * TILE, LANES), F32),
            dma((SUBSTEPS, 2)),
            dma((SUBSTEPS, 2)),
            dma((2,)),
            dma((2,)),
            dma((2,)),
            dma((2,)),
            pltpu.VMEM((6 * PLANNED, BLOCK), F32),
            pltpu.SMEM((BUCKETS + 1,), I32),
            pltpu.VMEM((DEVICES, RANKS), F32),
            pltpu.VMEM((11, FACE_ROWS, LANES), F32),
            pltpu.VMEM((3 * HALF, 2 * RANKS), F32),
            pltpu.VMEM((DEVICES, 4, RANKS), F32),
            pltpu.VMEM((BUCKETS, 6 * LANES, BUCKET), BF16),
            pltpu.VMEM((6 * HALF, 2 * RANKS), F32),
            dma,
            dma,
            dma,
        ],
        compiler_params=params(collective_id=0, has_side_effects=True),
        name="fields",
    )(les_state, les_density, far_state, far_density, counts, owner, cell, area, target)


def add_kernel(arrived_ref, stepped_ref, out, held, order, sums, starts):
    for part in range(3):
        high, low = halves(arrived_ref[pl.ds(part, DEVICES, stride=4), :])
        held[2 * part] = high
        held[2 * part + 1] = low
    target = arrived_ref[pl.ds(3, DEVICES, stride=4), :].astype(I32) - 1
    row, column = target >> 13, target & (COLS - 1)
    cell_row = ((row >> 3) * TILES + (column >> 7)) * TILE + (row & 7)
    bucket = jnp.where(target >= 0, cell_row >> 8, -1)
    held[6] = (cell_row & (BUCKET - 1)).astype(F32)
    held[7] = (column & (LANES - 1)).astype(F32)
    held[8], held[9] = block_and_lane(bucket_places(bucket, DEVICES, starts))
    order[...] = jnp.zeros_like(order)
    sums[...] = jnp.zeros_like(sums)
    by_lane = indices(BLOCK, LINE)
    by_block = indices(SORTED, LINE)
    wide = LINE // LANES

    @pl.loop(0, DEVICES * RANKS // LINE, unroll=2)
    def _(step):
        fact = [lines(held.at[i], step * wide, wide) for i in range(10)]
        order[...] += product(spread(by_block, fact[8], fact[:8]), one_hot(by_lane, fact[9]))

    by_row = indices(BUCKET, BLOCK)
    by_column = indices(LANES, BLOCK)

    @pl.loop(0, steps_of(starts))
    def _(step):
        for i in range(TOGETHER):
            block = step * TOGETHER + i
            fact = [order[pl.ds(part * SORTED + block, 1), :] for part in range(8)]
            bucket = bucket_of(block, starts)
            sums[bucket] += product(one_hot(by_row, fact[6]), spread(by_column, fact[7], fact[:6]))

    for part in range(3):
        high = slice(2 * part * LANES, (2 * part + 1) * LANES)
        low = slice((2 * part + 1) * LANES, (2 * part + 2) * LANES)
        for band in range(ROWS // TILE):
            rows = slice(band * TILE, (band + 1) * TILE)
            for block in range(TILES):
                first = (band * TILES + block) * TILE
                bucket, first = first // BUCKET, first % BUCKET
                columns = slice(block * LANES, (block + 1) * LANES)
                out[part, rows, columns] = stepped_ref[part, rows, columns] + (
                    sums[bucket, first : first + TILE, high]
                    + sums[bucket, first : first + TILE, low]
                )


def add(arrived, stepped):
    return pl.pallas_call(
        add_kernel,
        out_shape=jax.ShapeDtypeStruct((3, ROWS, COLS), F32),
        in_specs=[VMEM] * 2,
        out_specs=VMEM,
        scratch_shapes=[
            pltpu.VMEM((10, DEVICES, RANKS), F32),
            pltpu.VMEM((8 * SORTED, BLOCK), F32),
            pltpu.VMEM((BUCKETS, BUCKET, 6 * LANES), F32),
            pltpu.SMEM((BUCKETS + 1,), I32),
        ],
        compiler_params=params(),
        name="add",
    )(arrived, stepped)


def local(
    les_state,
    les_density,
    far_state,
    far_density,
    face_cell,
    face_area,
    face_owner,
    face_counts,
    face_target,
):
    cell, area, owner, target = (
        array.reshape(FACE_ROWS, LANES) for array in (face_cell, face_area, face_owner, face_target)
    )
    les_final, stepped, arrived = fields(
        les_state[0],
        les_density[0],
        far_state[0],
        far_density[0],
        face_counts,
        owner,
        cell,
        area,
        target,
    )
    far_final = add(arrived.reshape(4 * DEVICES, LANES), stepped)
    return les_final[None], far_final[None]


def solution(mesh):
    field = P("sec", None, "dom", None)
    density = P("sec", "dom", None)
    faces = P(("sec", "dom"))
    return jax.shard_map(
        local,
        mesh=mesh,
        in_specs=(field, density, field, density) + (faces,) * 5,
        out_specs=(field, field),
        check_vma=False,
    )
```

time: 115 us -> 98.8 us (0.86)
  Pallas kernels: 112 us -> 95.5 us
    pallas_call x4 -> x1, Pallas kernels: 92.6 us -> 76.9 us  [fields(): pl.pallas_call(fields_kernel, out_shape=(block, block, jax.ShapeDtypeStru...]
where the time goes in v4:
time: 98.8 us; the launch traced here: 98 us
  Pallas kernels  95.5 us (97%)
  between operations  1.3 us (1%)
  local copies, waits for them, and re-layouts  1.15 us (1%)
    pallas_call x1, Pallas kernels, fields(): pl.pallas_call(fields_kernel, out_shape=(block, block, jax.ShapeDtypeStru...  76.9 us
    pallas_call x1, Pallas kernels, add(): pl.pallas_call(add_kernel, out_shape=jax.ShapeDtypeStruct((3, ROWS, COLS)...  18.6 us

profile of v4, /device:TPU:1, one launch (start us, length us, event | category | flops | bytes accessed | tf_op | source)
XLA Modules:
  0.0 98.0 jit_solution(1327030869522619048)
XLA Ops:
  1.3 76.9 %fields.1 = (f32[3,16,8192]{2,1,0:T(8,128)}, f32[3,16,8192]{2,1,0:T(8,128)}, f32[128,4,128]{2,1,0:T(4,128)}) custom-call(f32[3,16,8192]{2,1,0:T(8,128)} %bitcast.11, f32[16,8192]{1,0:T(8,128)} %bitcast.15, f32[3,16,8192]{2,1,0:T(8,128)} %bitcast.12, f32[16,8192]{1,0:T(8,128)} %bitcast.16, s32[1]{0:T(128)S(6)} %copy.12.count_ref, s32[64,128]{1,0:T(8,128)} %bitcast.18, ...), custom_call_target="tpu_custom_call" | custom-call | tf_op jit(solution)/shard_map/fields/pallas_call | solution.py:635
  78.2 0.0 copy-start
  78.2 18.6 %add.1 = f32[3,16,8192]{2,1,0:T(8,128)} custom-call(f32[512,128]{1,0:T(8,128)} %bitcast.17, f32[3,16,8192]{2,1,0:T(8,128)} %get-tuple-element.7.stepped_ref), custom_call_target="tpu_custom_call" | custom-call | tf_op jit(solution)/shard_map/add/pallas_call | solution.py:721
  96.8 0.0 copy-done
  96.8 1.1 %copy.13 = f32[1,3,16,8192]{3,2,1,0:T(8,128)} copy(f32[1,3,16,8192]{3,2,1,0:T(8,128)S(1)} %bitcast.13) | data formatting | bytes 3145728
Async XLA Ops:
  78.2 18.6 %copy-start = (f32[3,16,8192]{2,1,0:T(8,128)S(1)}, f32[3,16,8192]{2,1,0:T(8,128)}, u32[]{:S(2)}) copy-start(f32[3,16,8192]{2,1,0:T(8,128)} %get-tuple-element.5) | copy-start | bytes 4718596

commit v5 on v4

--- a/solution.py
+++ b/solution.py
@@ -108,6 +108,13 @@
 
 def product(left, right):
     return lax.dot_general(left, right, (((1,), (1,)), ((), ())), preferred_element_type=F32)
+
+
+def folded(index, line, parts, right):
+    return product(
+        jnp.concatenate([spread(index, line, parts[0::2]), spread(index, line, parts[1::2])], axis=1),
+        jnp.concatenate([right, right], axis=1),
+    )
 
 
 def lines(ref, first, count):
@@ -244,7 +251,7 @@
     by_half = indices(HALF, BLOCK * TOGETHER)
     by_rank = indices(2 * RANKS, BLOCK * TOGETHER)
 
-    @pl.loop(0, (FACES // BLOCK + BUCKETS) // TOGETHER)
+    @pl.loop(0, (FACES // BLOCK + BUCKETS) // TOGETHER, unroll=3)
     def _(step):
         surface = []
         placed = []
@@ -328,17 +335,26 @@
     lane = lax.broadcasted_iota(I32, (TILES, LANES), 1)
     step = TIME_STEP / 12.0
 
-    devices = lax.axis_size("sec") * doms
-    me = lax.axis_index("sec") * doms + dom
+    sec = lax.axis_index("sec")
+    secs = lax.axis_size("sec")
+    devices = secs * doms
+    me = sec * doms + dom
     barrier = pltpu.get_barrier_semaphore()
 
-    def place(offset):
-        other = lax.rem(me + offset, devices)
-        return other, {"sec": other // doms, "dom": lax.rem(other, doms)}
-
-    @pl.loop(1, devices)
-    def _(offset):
-        pl.semaphore_signal(barrier, inc=1, device_id=place(offset)[1], device_id_type=MESH)
+    def for_others(act):
+        for ahead in range(secs):
+            there = lax.rem(sec + ahead, secs)
+
+            @pl.loop(0 if ahead else 1, doms, unroll=8 if ahead else doms - 1)
+            def _(along):
+                where = lax.rem(dom + along, doms)
+                act(there * doms + where, {"sec": there, "dom": where})
+
+    for_others(
+        lambda other, where: pl.semaphore_signal(
+            barrier, inc=1, device_id=where, device_id_type=MESH
+        )
+    )
 
     def remote(ref, first, count, landing, sems, where):
         return pltpu.make_async_remote_copy(
@@ -542,16 +558,22 @@
 
         @pl.when(has_up)
         def _():
+            down_copy(sub).wait_recv()
             if sub == 0:
-                down_copy(0).wait_recv()
                 inverse_down().wait_recv()
+            else:
+                advance_rows(sub - 1, -4, -1)
+                smooth_rows(sub - 1, -3, 0, own=False)
             put_advanced(-1, advance(sub, -1))
 
         @pl.when(has_down)
         def _():
+            up_copy(sub).wait_recv()
             if sub == 0:
-                up_copy(0).wait_recv()
                 inverse_up().wait_recv()
+            else:
+                advance_rows(sub - 1, ROWS + 1, ROWS + 4)
+                smooth_rows(sub - 1, ROWS, ROWS + 3, own=False)
             put_advanced(ROWS, advance(sub, ROWS))
 
         advance_rows(sub, 0, 2)
@@ -559,28 +581,12 @@
         smooth_rows(sub, 0, 3)
         smooth_rows(sub, ROWS - 3, ROWS)
 
-        if sub + 1 < SUBSTEPS:
-
-            @pl.when(has_up)
-            def _():
-                down_copy(sub + 1).wait_recv()
-                advance_rows(sub, -4, -1)
-                smooth_rows(sub, -3, 0, own=False)
-
-            @pl.when(has_down)
-            def _():
-                up_copy(sub + 1).wait_recv()
-                advance_rows(sub, ROWS + 1, ROWS + 4)
-                smooth_rows(sub, ROWS, ROWS + 3, own=False)
-
     pick_faces(total_out, order, starts, targets, ready, turned, slots)
     own = pltpu.make_async_copy(ready.at[me], arrived.at[me], local_sem)
     own.start()
 
-    @pl.loop(1, devices)
-    def _(offset):
-        other, where = place(offset)
-        pltpu.make_async_remote_copy(
+    for_others(
+        lambda other, where: pltpu.make_async_remote_copy(
             src_ref=ready.at[other],
             dst_ref=arrived.at[me],
             send_sem=faces_send,
@@ -588,6 +594,7 @@
             device_id=where,
             device_id_type=MESH,
         ).start()
+    )
 
     write_tiles(
         lambda row, part, reg: state[SUBSTEPS, row + 6, part, reg * TILE : (reg + 1) * TILE, :],
@@ -670,9 +677,9 @@
 
 def add_kernel(arrived_ref, stepped_ref, out, held, order, sums, starts):
     for part in range(3):
-        high, low = halves(arrived_ref[pl.ds(part, DEVICES, stride=4), :])
-        held[2 * part] = high
-        held[2 * part + 1] = low
+        held[2 * part], held[2 * part + 1] = halves(
+            arrived_ref[pl.ds(part, DEVICES, stride=4), :]
+        )
     target = arrived_ref[pl.ds(3, DEVICES, stride=4), :].astype(I32) - 1
     row, column = target >> 13, target & (COLS - 1)
     cell_row = ((row >> 3) * TILES + (column >> 7)) * TILE + (row & 7)
@@ -686,7 +693,7 @@
     by_block = indices(SORTED, LINE)
     wide = LINE // LANES
 
-    @pl.loop(0, DEVICES * RANKS // LINE, unroll=2)
+    @pl.loop(0, DEVICES * RANKS // LINE, unroll=4)
     def _(step):
         fact = [lines(held.at[i], step * wide, wide) for i in range(10)]
         order[...] += product(spread(by_block, fact[8], fact[:8]), one_hot(by_lane, fact[9]))
@@ -698,23 +705,24 @@
     def _(step):
         for i in range(TOGETHER):
             block = step * TOGETHER + i
-            fact = [order[pl.ds(part * SORTED + block, 1), :] for part in range(8)]
-            bucket = bucket_of(block, starts)
-            sums[bucket] += product(one_hot(by_row, fact[6]), spread(by_column, fact[7], fact[:6]))
+            *parts, row, column = (order[pl.ds(part * SORTED + block, 1), :] for part in range(8))
+            sums[bucket_of(block, starts)] += folded(by_column, column, parts, one_hot(by_row, row))
 
     for part in range(3):
-        high = slice(2 * part * LANES, (2 * part + 1) * LANES)
-        low = slice((2 * part + 1) * LANES, (2 * part + 2) * LANES)
-        for band in range(ROWS // TILE):
-            rows = slice(band * TILE, (band + 1) * TILE)
-            for block in range(TILES):
-                first = (band * TILES + block) * TILE
-                bucket, first = first // BUCKET, first % BUCKET
-                columns = slice(block * LANES, (block + 1) * LANES)
-                out[part, rows, columns] = stepped_ref[part, rows, columns] + (
-                    sums[bucket, first : first + TILE, high]
-                    + sums[bucket, first : first + TILE, low]
-                )
+        for bucket in range(BUCKETS):
+            for half in range(BUCKET // LANES):
+                cells = sums[
+                    bucket,
+                    part * LANES : (part + 1) * LANES,
+                    half * LANES : (half + 1) * LANES,
+                ].T
+                for tile in range(LANES // TILE):
+                    number = (bucket * BUCKET + half * LANES) // TILE + tile
+                    rows = slice(number // TILES * TILE, (number // TILES + 1) * TILE)
+                    columns = slice(number % TILES * LANES, (number % TILES + 1) * LANES)
+                    out[part, rows, columns] = (
+                        stepped_ref[part, rows, columns] + cells[tile * TILE : (tile + 1) * TILE]
+                    )
 
 
 def add(arrived, stepped):
@@ -726,7 +734,7 @@
         scratch_shapes=[
             pltpu.VMEM((10, DEVICES, RANKS), F32),
             pltpu.VMEM((8 * SORTED, BLOCK), F32),
-            pltpu.VMEM((BUCKETS, BUCKET, 6 * LANES), F32),
+            pltpu.VMEM((BUCKETS, 3 * LANES, BUCKET), F32),
             pltpu.SMEM((BUCKETS + 1,), I32),
         ],
         compiler_params=params(),

time: 98.8 us -> 90.5 us (0.916)
  the two profiles are of different devices: /device:TPU:1 before, /device:TPU:51 now
where the time goes in v5:
time: 90.5 us; the launch traced here: 90.4 us
  Pallas kernels  87.9 us (97%)
  between operations  1.3 us (1%)
  local copies, waits for them, and re-layouts  1.15 us (1%)
    pallas_call x1, Pallas kernels, fields(): pl.pallas_call(fields_kernel, out_shape=(block, block, jax.ShapeDtypeStru...  65.2 us
    pallas_call x1, Pallas kernels, add(): pl.pallas_call(add_kernel, out_shape=jax.ShapeDtypeStruct((3, ROWS, COLS)...  22.7 us

profile of v5, /device:TPU:51, one launch (start us, length us, event | category | flops | bytes accessed | tf_op | source)
XLA Modules:
  0.0 90.4 jit_solution(11526653257785334211)
XLA Ops:
  1.3 65.2 %fields.1 = (f32[3,16,8192]{2,1,0:T(8,128)}, f32[3,16,8192]{2,1,0:T(8,128)}, f32[128,4,128]{2,1,0:T(4,128)}) custom-call(f32[3,16,8192]{2,1,0:T(8,128)} %bitcast.11, f32[16,8192]{1,0:T(8,128)} %bitcast.15, f32[3,16,8192]{2,1,0:T(8,128)} %bitcast.12, f32[16,8192]{1,0:T(8,128)} %bitcast.16, s32[1]{0:T(128)S(6)} %copy.12.count_ref, s32[64,128]{1,0:T(8,128)} %bitcast.18, ...), custom_call_target="tpu_custom_call" | custom-call | tf_op jit(solution)/shard_map/fields/pallas_call | solution.py:642
  66.5 0.0 copy-start
  66.5 22.7 %add.1 = f32[3,16,8192]{2,1,0:T(8,128)} custom-call(f32[512,128]{1,0:T(8,128)} %bitcast.17, f32[3,16,8192]{2,1,0:T(8,128)} %get-tuple-element.7.stepped_ref), custom_call_target="tpu_custom_call" | custom-call | tf_op jit(solution)/shard_map/add/pallas_call | solution.py:729
  89.2 0.0 copy-done
  89.2 1.1 %copy.13 = f32[1,3,16,8192]{3,2,1,0:T(8,128)} copy(f32[1,3,16,8192]{3,2,1,0:T(8,128)S(1)} %bitcast.13) | data formatting | bytes 3145728
Async XLA Ops:
  66.5 22.7 %copy-start = (f32[3,16,8192]{2,1,0:T(8,128)S(1)}, f32[3,16,8192]{2,1,0:T(8,128)}, u32[]{:S(2)}) copy-start(f32[3,16,8192]{2,1,0:T(8,128)} %get-tuple-element.5) | copy-start | bytes 4718596

commit v6 on v5

--- a/solution.py
+++ b/solution.py
@@ -18,6 +18,7 @@
 ROWS = 16
 COLS = 8192
 TILES = COLS // LANES
+GREETINGS = SUBSTEPS + 1
 REGS = TILES // TILE
 FACES = 8192
 FACE_ROWS = FACES // LANES
@@ -27,6 +28,7 @@
 
 MESH = pl.DeviceIdType.MESH
 VMEM = pl.BlockSpec(memory_space=pltpu.VMEM)
+HBM = pl.BlockSpec(memory_space=pl.ANY)
 SMEM = pl.BlockSpec(memory_space=pltpu.SMEM)
 F32 = jnp.float32
 BF16 = jnp.bfloat16
@@ -83,7 +85,8 @@
 TOGETHER = 4
 HALF = DEVICES // 2
 PLANNED = 48
-SORTED = 80
+GROUPS = 2
+SORTED = 48
 
 
 def halves(values):
@@ -251,7 +254,7 @@
     by_half = indices(HALF, BLOCK * TOGETHER)
     by_rank = indices(2 * RANKS, BLOCK * TOGETHER)
 
-    @pl.loop(0, (FACES // BLOCK + BUCKETS) // TOGETHER, unroll=3)
+    @pl.loop(0, (FACES // BLOCK + BUCKETS) // TOGETHER, unroll=9)
     def _(step):
         surface = []
         placed = []
@@ -301,6 +304,9 @@
     les_out,
     stepped_out,
     arrived,
+    les_tiles,
+    stepped_tiles,
+    out_sem,
     total_out,
     state,
     advanced,
@@ -325,6 +331,7 @@
     local_sem,
     faces_send,
     faces_recv,
+    greeted,
 ):
     dom = lax.axis_index("dom")
     doms = lax.axis_size("dom")
@@ -350,11 +357,22 @@
                 where = lax.rem(dom + along, doms)
                 act(there * doms + where, {"sec": there, "dom": where})
 
-    for_others(
-        lambda other, where: pl.semaphore_signal(
-            barrier, inc=1, device_id=where, device_id_type=MESH
-        )
-    )
+    def greet(distance, semaphore):
+        for by in (distance, devices - distance):
+            other = lax.rem(me + by, devices)
+            pl.semaphore_signal(
+                semaphore,
+                inc=1,
+                device_id={"sec": other // doms, "dom": lax.rem(other, doms)},
+                device_id_type=MESH,
+            )
+
+    def pass_on(number):
+        pl.semaphore_wait(greeted.at[number], 2)
+        if number + 1 < GREETINGS:
+            greet(2 << number, greeted.at[number + 1])
+
+    greet(1, barrier)
 
     def remote(ref, first, count, landing, sems, where):
         return pltpu.make_async_remote_copy(
@@ -498,7 +516,8 @@
     convert_state(les_ref, state.at[0], 6)
     convert_density(les_density_ref, inverse, 4)
 
-    pl.semaphore_wait(barrier, devices - 1)
+    pl.semaphore_wait(barrier, 2)
+    greet(1, greeted.at[0])
 
     @pl.when(has_up)
     def _():
@@ -535,6 +554,8 @@
             @pl.when(has_down)
             def _():
                 far_down().start()
+
+        pass_on(sub)
 
         if sub == 0:
             convert_state(far_ref, far, 2)
@@ -582,6 +603,7 @@
         smooth_rows(sub, ROWS - 3, ROWS)
 
     pick_faces(total_out, order, starts, targets, ready, turned, slots)
+    pass_on(GREETINGS - 1)
     own = pltpu.make_async_copy(ready.at[me], arrived.at[me], local_sem)
     own.start()
 
@@ -598,8 +620,10 @@
 
     write_tiles(
         lambda row, part, reg: state[SUBSTEPS, row + 6, part, reg * TILE : (reg + 1) * TILE, :],
-        les_out,
-    )
+        les_tiles,
+    )
+    les_copy = pltpu.make_async_copy(les_tiles, les_out, out_sem.at[0])
+    les_copy.start()
 
     @pl.when(has_up)
     def _():
@@ -613,8 +637,10 @@
     loop(ROWS - 2, ROWS, far_row)
     write_tiles(
         lambda row, part, reg: far[row + ROWS + 6, part, reg * TILE : (reg + 1) * TILE, :],
-        stepped_out,
-    )
+        stepped_tiles,
+    )
+    stepped_copy = pltpu.make_async_copy(stepped_tiles, stepped_out, out_sem.at[1])
+    stepped_copy.start()
 
     @pl.when(has_up)
     def _():
@@ -631,6 +657,8 @@
         far_down().wait_send()
 
     own.wait()
+    les_copy.wait()
+    stepped_copy.wait()
     all_but_one = pl.ds(0, devices - 1)
     pltpu.make_async_copy(arrived.at[all_but_one], arrived.at[all_but_one], faces_recv).wait()
     pltpu.make_async_copy(ready.at[all_but_one], ready.at[all_but_one], faces_send).wait()
@@ -643,8 +671,11 @@
         fields_kernel,
         out_shape=(block, block, jax.ShapeDtypeStruct((DEVICES, 4, RANKS), F32)),
         in_specs=[VMEM] * 4 + [SMEM] + [VMEM] * 4,
-        out_specs=(VMEM,) * 3,
+        out_specs=(HBM, HBM, VMEM),
         scratch_shapes=[
+            pltpu.VMEM((3, ROWS, COLS), F32),
+            pltpu.VMEM((3, ROWS, COLS), F32),
+            dma((2,)),
             pltpu.VMEM((3, ROWS, TILES, LANES), F32),
             pltpu.VMEM((SUBSTEPS + 1, ROWS + 12, 3, TILES, LANES), F32),
             pltpu.VMEM((ROWS + 8, 3, TILES, LANES), F32),
@@ -669,6 +700,7 @@
             dma,
             dma,
             dma,
+            pltpu.SemaphoreType.REGULAR((GREETINGS,)),
         ],
         compiler_params=params(collective_id=0, has_side_effects=True),
         name="fields",
@@ -686,27 +718,39 @@
     bucket = jnp.where(target >= 0, cell_row >> 8, -1)
     held[6] = (cell_row & (BUCKET - 1)).astype(F32)
     held[7] = (column & (LANES - 1)).astype(F32)
-    held[8], held[9] = block_and_lane(bucket_places(bucket, DEVICES, starts))
+    share = DEVICES // GROUPS
+    for group in range(GROUPS):
+        rows = slice(group * share, (group + 1) * share)
+        held[8, rows], held[9, rows] = block_and_lane(
+            bucket_places(bucket[rows], share, starts.at[group])
+        )
     order[...] = jnp.zeros_like(order)
     sums[...] = jnp.zeros_like(sums)
     by_lane = indices(BLOCK, LINE)
     by_block = indices(SORTED, LINE)
     wide = LINE // LANES
 
-    @pl.loop(0, DEVICES * RANKS // LINE, unroll=4)
-    def _(step):
-        fact = [lines(held.at[i], step * wide, wide) for i in range(10)]
-        order[...] += product(spread(by_block, fact[8], fact[:8]), one_hot(by_lane, fact[9]))
+    for group in range(GROUPS):
+
+        @pl.loop(0, share // wide, unroll=4)
+        def _(step):
+            fact = [lines(held.at[i], group * share + step * wide, wide) for i in range(10)]
+            order[group] += product(spread(by_block, fact[8], fact[:8]), one_hot(by_lane, fact[9]))
 
     by_row = indices(BUCKET, BLOCK)
     by_column = indices(LANES, BLOCK)
 
-    @pl.loop(0, steps_of(starts))
-    def _(step):
-        for i in range(TOGETHER):
-            block = step * TOGETHER + i
-            *parts, row, column = (order[pl.ds(part * SORTED + block, 1), :] for part in range(8))
-            sums[bucket_of(block, starts)] += folded(by_column, column, parts, one_hot(by_row, row))
+    for group in range(GROUPS):
+
+        @pl.loop(0, steps_of(starts.at[group]))
+        def _(step):
+            for i in range(TOGETHER):
+                block = step * TOGETHER + i
+                *parts, row, column = (
+                    order[group, pl.ds(part * SORTED + block, 1), :] for part in range(8)
+                )
+                here = folded(by_column, column, parts, one_hot(by_row, row))
+                sums[bucket_of(block, starts.at[group])] += here
 
     for part in range(3):
         for bucket in range(BUCKETS):
@@ -733,9 +777,9 @@
         out_specs=VMEM,
         scratch_shapes=[
             pltpu.VMEM((10, DEVICES, RANKS), F32),
-            pltpu.VMEM((8 * SORTED, BLOCK), F32),
+            pltpu.VMEM((GROUPS, 8 * SORTED, BLOCK), F32),
             pltpu.VMEM((BUCKETS, 3 * LANES, BUCKET), F32),
-            pltpu.SMEM((BUCKETS + 1,), I32),
+            pltpu.SMEM((GROUPS, BUCKETS + 1), I32),
         ],
         compiler_params=params(),
         name="add",

time: 90.5 us -> 84.3 us (0.931)
  the two profiles are of different devices: /device:TPU:51 before, /device:TPU:1 now
where the time goes in v6:
time: 84.3 us; the launch traced here: 84.1 us
  Pallas kernels  81.7 us (97%)
  between operations  1.3 us (2%)
  local copies, waits for them, and re-layouts  1.15 us (1%)
    pallas_call x1, Pallas kernels, fields(): pl.pallas_call(fields_kernel, out_shape=(block, block, jax.ShapeDtypeStru...  65.4 us
    pallas_call x1, Pallas kernels, add(): pl.pallas_call(add_kernel, out_shape=jax.ShapeDtypeStruct((3, ROWS, COLS)...  16.3 us

profile of v6, /device:TPU:1, one launch (start us, length us, event | category | flops | bytes accessed | tf_op | source)
XLA Modules:
  0.0 84.1 jit_solution(15598794495874969379)
XLA Ops:
  1.3 65.4 %fields.1 = (f32[3,16,8192]{2,1,0:T(8,128)}, f32[3,16,8192]{2,1,0:T(8,128)}, f32[128,4,128]{2,1,0:T(4,128)}) custom-call(f32[3,16,8192]{2,1,0:T(8,128)} %bitcast.11, f32[16,8192]{1,0:T(8,128)} %bitcast.15, f32[3,16,8192]{2,1,0:T(8,128)} %bitcast.12, f32[16,8192]{1,0:T(8,128)} %bitcast.16, s32[1]{0:T(128)S(6)} %copy.12.count_ref, s32[64,128]{1,0:T(8,128)} %bitcast.18, ...), custom_call_target="tpu_custom_call" | custom-call | tf_op jit(solution)/shard_map/fields/pallas_call | solution.py:670
  66.7 0.0 copy-start
  66.7 16.3 %add.1 = f32[3,16,8192]{2,1,0:T(8,128)} custom-call(f32[512,128]{1,0:T(8,128)} %bitcast.17, f32[3,16,8192]{2,1,0:T(8,128)} %get-tuple-element.7.stepped_ref), custom_call_target="tpu_custom_call" | custom-call | tf_op jit(solution)/shard_map/add/pallas_call | solution.py:773
  83.0 0.0 copy-done
  83.0 1.1 %copy.13 = f32[1,3,16,8192]{3,2,1,0:T(8,128)} copy(f32[1,3,16,8192]{3,2,1,0:T(8,128)S(1)} %bitcast.13) | data formatting | bytes 3145728
Async XLA Ops:
  66.7 16.3 %copy-start = (f32[3,16,8192]{2,1,0:T(8,128)S(1)}, f32[3,16,8192]{2,1,0:T(8,128)}, u32[]{:S(2)}) copy-start(f32[3,16,8192]{2,1,0:T(8,128)} %get-tuple-element.5) | copy-start | bytes 4718596

commit v7 on v6

--- a/solution.py
+++ b/solution.py
@@ -707,7 +707,25 @@
     )(les_state, les_density, far_state, far_density, counts, owner, cell, area, target)
 
 
-def add_kernel(arrived_ref, stepped_ref, out, held, order, sums, starts):
+def add_kernel(
+    arrived_ref,
+    les_hbm,
+    stepped_hbm,
+    les_out,
+    out,
+    stepped_ref,
+    les_held,
+    held,
+    order,
+    sums,
+    starts,
+    copy_sem,
+):
+    les_copy = pltpu.make_async_copy(les_hbm, les_held, copy_sem.at[0])
+    les_store = pltpu.make_async_copy(les_held, les_out, copy_sem.at[2])
+    stepped_copy = pltpu.make_async_copy(stepped_hbm, stepped_ref, copy_sem.at[1])
+    stepped_copy.start()
+    les_copy.start()
     for part in range(3):
         held[2 * part], held[2 * part + 1] = halves(
             arrived_ref[pl.ds(part, DEVICES, stride=4), :]
@@ -732,11 +750,13 @@
 
     for group in range(GROUPS):
 
-        @pl.loop(0, share // wide, unroll=4)
+        @pl.loop(0, share // wide, unroll=8)
         def _(step):
             fact = [lines(held.at[i], group * share + step * wide, wide) for i in range(10)]
             order[group] += product(spread(by_block, fact[8], fact[:8]), one_hot(by_lane, fact[9]))
 
+    les_copy.wait()
+    les_store.start()
     by_row = indices(BUCKET, BLOCK)
     by_column = indices(LANES, BLOCK)
 
@@ -752,6 +772,7 @@
                 here = folded(by_column, column, parts, one_hot(by_row, row))
                 sums[bucket_of(block, starts.at[group])] += here
 
+    stepped_copy.wait()
     for part in range(3):
         for bucket in range(BUCKETS):
             for half in range(BUCKET // LANES):
@@ -767,23 +788,27 @@
                     out[part, rows, columns] = (
                         stepped_ref[part, rows, columns] + cells[tile * TILE : (tile + 1) * TILE]
                     )
-
-
-def add(arrived, stepped):
+    les_store.wait()
+
+
+def add(arrived, les_final, stepped):
     return pl.pallas_call(
         add_kernel,
-        out_shape=jax.ShapeDtypeStruct((3, ROWS, COLS), F32),
-        in_specs=[VMEM] * 2,
-        out_specs=VMEM,
+        out_shape=(jax.ShapeDtypeStruct((3, ROWS, COLS), F32),) * 2,
+        in_specs=[VMEM, HBM, HBM],
+        out_specs=(HBM, VMEM),
         scratch_shapes=[
+            pltpu.VMEM((3, ROWS, COLS), F32),
+            pltpu.VMEM((3, ROWS, COLS), F32),
             pltpu.VMEM((10, DEVICES, RANKS), F32),
             pltpu.VMEM((GROUPS, 8 * SORTED, BLOCK), F32),
             pltpu.VMEM((BUCKETS, 3 * LANES, BUCKET), F32),
             pltpu.SMEM((GROUPS, BUCKETS + 1), I32),
+            pltpu.SemaphoreType.DMA((3,)),
         ],
         compiler_params=params(),
         name="add",
-    )(arrived, stepped)
+    )(arrived, les_final, stepped)
 
 
 def local(
@@ -811,7 +836,7 @@
         area,
         target,
     )
-    far_final = add(arrived.reshape(4 * DEVICES, LANES), stepped)
+    les_final, far_final = add(arrived.reshape(4 * DEVICES, LANES), les_final, stepped)
     return les_final[None], far_final[None]
 
 

time: 84.3 us -> 82.9 us (0.983)
  the two profiles are of different devices: /device:TPU:1 before, /device:TPU:9 now
where the time goes in v7:
time: 82.9 us; the launch traced here: 84 us
  Pallas kernels  82.6 us (100%)
  between operations  1.45 us (2%)
    pallas_call x1, Pallas kernels, fields(): pl.pallas_call(fields_kernel, out_shape=(block, block, jax.ShapeDtypeStru...  63.5 us
    pallas_call x1, Pallas kernels, add(): pl.pallas_call(add_kernel, out_shape=(jax.ShapeDtypeStruct((3, ROWS, COLS...  19.1 us

profile of v7, /device:TPU:9, one launch (start us, length us, event | category | flops | bytes accessed | tf_op | source)
XLA Modules:
  0.0 84.0 jit_solution(4689264665811189824)
XLA Ops:
  1.3 63.5 %fields.1 = (f32[3,16,8192]{2,1,0:T(8,128)}, f32[3,16,8192]{2,1,0:T(8,128)}, f32[128,4,128]{2,1,0:T(4,128)}) custom-call(f32[3,16,8192]{2,1,0:T(8,128)} %bitcast.11, f32[16,8192]{1,0:T(8,128)} %bitcast.13, f32[3,16,8192]{2,1,0:T(8,128)} %bitcast.12, f32[16,8192]{1,0:T(8,128)} %bitcast.14, s32[1]{0:T(128)S(6)} %copy.11.count_ref, s32[64,128]{1,0:T(8,128)} %bitcast.16, ...), custom_call_target="tpu_custom_call" | custom-call | tf_op jit(solution)/shard_map/fields/pallas_call | solution.py:670
  64.7 19.1 %add.1 = (f32[3,16,8192]{2,1,0:T(8,128)}, f32[3,16,8192]{2,1,0:T(8,128)}) custom-call(f32[512,128]{1,0:T(8,128)} %bitcast.15, f32[3,16,8192]{2,1,0:T(8,128)} %get-tuple-element.8.les_hbm, f32[3,16,8192]{2,1,0:T(8,128)} %get-tuple-element.9.stepped_hbm), custom_call_target="tpu_custom_call" | custom-call | tf_op jit(solution)/shard_map/add/pallas_call | solution.py:795
